TPU v7x, 32 devices: a whole 2x2x4 slice. The times are simulated.
32 devices in a mesh: blk: 8 (over y, x, core), ch: 4 (over z).
Axes of the slice: x: 2, y: 2, z: 4, core: 2. Of those that a mesh axis runs over, the one named last changes fastest.
Arguments:
- block_input: bfloat16 [2, 64, 64, 512], P(None, 'blk', None, 'ch'), may hold values from -18 to 18
- cotangent: bfloat16 [2, 64, 64, 512], P(None, 'blk', None, 'ch'), may hold values from -6 to 6
- image_embed: float32 [2, 2048], replicated, may hold values from -6 to 6
- timesteps: int32 [2], replicated, may hold values from 0 to 999
- text_len: int32 [2], replicated, may hold values from 5 to 256, as said below
- context: bfloat16 [2, 260, 2048], P(None, None, 'ch'), may hold values from -6 to 6
- conv1_weight: bfloat16 [3, 3, 512, 512], P(None, None, None, 'ch'), may hold values from -0.09375 to 0.09375
- conv2_weight: bfloat16 [3, 3, 512, 512], P(None, None, None, 'ch'), may hold values from -0.09375 to 0.09375
- embed_weight: bfloat16 [2048, 2, 512], P(None, None, 'ch'), may hold values from -0.125 to 0.125
- embed_bias: float32 [2, 512], P(None, 'ch'), may hold values from -2 to 2
- norm1_gain: float32 [512], P('ch'), may hold values from 0.5 to 1.5
- norm1_bias: float32 [512], P('ch'), may hold values from -2 to 2
- norm2_gain: float32 [512], P('ch'), may hold values from 0.5 to 1.5
- norm2_bias: float32 [512], P('ch'), may hold values from -2 to 2
- norm3_gain: float32 [512], P('ch'), may hold values from 0.5 to 1.5
- norm3_bias: float32 [512], P('ch'), may hold values from -2 to 2
- qkv_weight: bfloat16 [512, 3, 512], P(None, None, 'ch'), may hold values from -0.25 to 0.25
- out_weight: bfloat16 [512, 512], P('ch'), may hold values from -2 to 2
- ctx_weight: bfloat16 [2048, 2, 512], P('ch'), may hold values from -0.125 to 0.125
Outputs:
- block_output: bfloat16 [2, 64, 64, 512], P(None, 'blk', None, 'ch')
- input_grad: float32 [2, 64, 64, 512], P(None, 'blk', None, 'ch')
- conv1_grad: float32 [3, 3, 512, 512], P(None, None, None, 'ch')
- conv2_grad: float32 [3, 3, 512, 512], P(None, None, None, 'ch')
- embed_weight_grad: float32 [2048, 2, 512], P(None, None, 'ch')
- embed_bias_grad: float32 [2, 512], P(None, 'ch')
- norm1_gain_grad: float32 [512], P('ch')
- norm1_bias_grad: float32 [512], P('ch')
- norm2_gain_grad: float32 [512], P('ch')
- norm2_bias_grad: float32 [512], P('ch')
- norm3_gain_grad: float32 [512], P('ch')
- norm3_bias_grad: float32 [512], P('ch')
- qkv_grad: float32 [512, 3, 512], P(None, None, 'ch')
- out_grad: float32 [512, 512], P('ch')
- ctx_grad: float32 [2048, 2, 512], P('ch')
Inputs may be any that keep to these rules, and one draw needn't show every extreme that they name: `text_len`: in every draw one image's text has exactly 256 tokens.
All inputs are finite; a program needn't handle non-finite values.
Results may differ from a plain program's by a relative error of at most 0.024.
Values may be sent and summed in bfloat16 or wider, within the bound.
No kernel may reach another device: no remote copies, remote signals or barrier semaphores. Data moves between devices by JAX's collectives and lax.ppermute only.
A program may use at most 192 MiB of HBM per device.

v0:
```python
import math

import jax
import jax.numpy as jnp
from jax import lax
from jax.sharding import PartitionSpec as P

HEAD = 64
GROUPS = 32
CLIPTOK = 4


def with_halo(block, sides, width):
    for axis, dim in sides:
        count = lax.axis_size(axis)
        forward = [(i, i + 1) for i in range(count - 1)]
        backward = [(target, source) for source, target in forward]
        low = lax.ppermute(
            lax.slice_in_dim(block, block.shape[dim] - width, None, axis=dim), axis, forward
        )
        high = lax.ppermute(lax.slice_in_dim(block, 0, width, axis=dim), axis, backward)
        block = jnp.concatenate([low, block, high], axis=dim)
    return block


def silu_slope(field):
    sigma = jax.nn.sigmoid(field)
    return sigma * (1.0 + field * (1.0 - sigma))


def embed_features(timesteps, image_embed):
    half_width = image_embed.shape[1] // 2
    freqs = jnp.exp(-math.log(10000.0) * jnp.arange(half_width, dtype=jnp.float32) / half_width)
    angles = timesteps.astype(jnp.float32)[:, None] * freqs[None, :]
    return jax.nn.silu(jnp.concatenate([jnp.cos(angles), jnp.sin(angles)], axis=1) + image_embed)


def body(
    block_input,
    cotangent,
    image_embed,
    timesteps,
    text_len,
    context,
    conv1_weight,
    conv2_weight,
    embed_weight,
    embed_bias,
    norm1_gain,
    norm1_bias,
    norm2_gain,
    norm2_bias,
    norm3_gain,
    norm3_bias,
    qkv_weight,
    out_weight,
    ctx_weight,
):
    images, row_count, col_count, local_width = block_input.shape
    channels = qkv_weight.shape[0]
    group_size = channels // GROUPS
    group_cells = row_count * lax.axis_size("blk") * col_count * group_size
    heads_here = local_width // HEAD
    ctx_len = context.shape[1]
    pixels = row_count * col_count
    key_block = 512
    block_total = pixels * lax.axis_size("blk") // key_block
    score_scale = 1.0 / math.sqrt(HEAD)

    def group_means(first, second):
        first_g = first.reshape(images, -1, group_size).sum(axis=2)
        second_g = second.reshape(images, -1, group_size).sum(axis=2)
        total_first, total_second = lax.psum((first_g, second_g), "blk")
        wide_first = jnp.repeat(total_first, group_size, axis=1) / group_cells
        wide_second = jnp.repeat(total_second, group_size, axis=1) / group_cells
        return (wide_first[:, None, None, :], wide_second[:, None, None, :])

    def normalize(field):
        mean_val, mean_sq = group_means(
            jnp.sum(field, axis=(1, 2)), jnp.sum(field * field, axis=(1, 2))
        )
        inv_std = lax.rsqrt(mean_sq - mean_val * mean_val + 1e-05)
        return ((field - mean_val) * inv_std, inv_std)

    def norm_back(d_hat, normed, inv_std):
        mean_one, mean_two = group_means(
            jnp.sum(d_hat, axis=(1, 2)), jnp.sum(d_hat * normed, axis=(1, 2))
        )
        return (d_hat - mean_one - normed * mean_two) * inv_std

    def row_margin(field):
        return with_halo(field, (("blk", 1),), 1)

    def all_channels(field):
        return lax.all_gather(field, "ch", axis=3, tiled=True)

    def conv_input(field):
        return jnp.pad(row_margin(all_channels(field)), ((0, 0), (0, 0), (1, 1), (0, 0)))

    def conv_apply(padded, weight):
        total = jnp.zeros((images, row_count, col_count, weight.shape[3]), jnp.float32)
        for tap_row in range(3):
            for tap_col in range(3):
                window = padded[:, tap_row : tap_row + row_count, tap_col : tap_col + col_count]
                total = total + jnp.einsum(
                    "irwc,cd->irwd",
                    window,
                    weight[tap_row, tap_col],
                    preferred_element_type=jnp.float32,
                )
        return total

    def conv_back(padded, grad_out, weight):
        grad_pad = jnp.pad(row_margin(grad_out), ((0, 0), (0, 0), (1, 1), (0, 0)))
        term = jnp.zeros((images, row_count, col_count, channels), jnp.float32)
        taps = []
        for tap_row in range(3):
            for tap_col in range(3):
                window = padded[:, tap_row : tap_row + row_count, tap_col : tap_col + col_count]
                taps.append(
                    jnp.einsum(
                        "irwc,irwd->cd", window, grad_out, preferred_element_type=jnp.float32
                    )
                )
                back_window = grad_pad[
                    :, 2 - tap_row : 2 - tap_row + row_count, 2 - tap_col : 2 - tap_col + col_count
                ]
                term = term + jnp.einsum(
                    "irwd,cd->irwc",
                    back_window,
                    weight[tap_row, tap_col],
                    preferred_element_type=jnp.float32,
                )
        weight_grad = jnp.stack(taps).reshape(3, 3, channels, local_width)
        return (
            weight_grad,
            lax.psum_scatter(
                term.astype(jnp.bfloat16), "ch", scatter_dimension=3, tiled=True
            ).astype(jnp.float32),
        )

    emb_act = embed_features(timesteps, image_embed).astype(jnp.bfloat16)
    scale_shift = (
        jnp.einsum("ie,esc->isc", emb_act, embed_weight, preferred_element_type=jnp.float32)
        + embed_bias
    )
    emb_scale = scale_shift[:, 0][:, None, None, :]
    emb_shift = scale_shift[:, 1][:, None, None, :]

    def res_forward(input_f):
        hat_one, inv_one = normalize(input_f)
        pre_one = hat_one * norm1_gain + norm1_bias
        pad_one = conv_input(jax.nn.silu(pre_one).astype(jnp.bfloat16))
        hidden = conv_apply(pad_one, conv1_weight)
        hat_two, inv_two = normalize(hidden)
        base_two = hat_two * norm2_gain + norm2_bias
        pre_two = base_two * (1.0 + emb_scale) + emb_shift
        pad_two = conv_input(jax.nn.silu(pre_two).astype(jnp.bfloat16))
        return (
            hat_one,
            inv_one,
            pre_one,
            pad_one,
            hat_two,
            inv_two,
            base_two,
            pre_two,
            pad_two,
            conv_apply(pad_two, conv2_weight),
        )

    input_f = block_input.astype(jnp.float32)
    resid = input_f + res_forward(input_f)[9]
    hat_three, inv_three = normalize(resid)
    act_three = (hat_three * norm3_gain + norm3_bias).astype(jnp.bfloat16)
    act_all = all_channels(act_three).reshape(images, pixels, channels)
    qkv = jnp.einsum(
        "ipc,ctd->iptd", act_all, qkv_weight, preferred_element_type=jnp.float32
    ).astype(jnp.bfloat16)
    query = qkv[:, :, 0].reshape(images, pixels, heads_here, HEAD)
    kv_local = jnp.transpose(qkv[:, :, 1:], (1, 0, 2, 3))
    ctx_term = jnp.einsum("itx,xsc->itsc", context, ctx_weight, preferred_element_type=jnp.float32)
    ctx_kv = lax.psum_scatter(ctx_term.astype(jnp.bfloat16), "ch", scatter_dimension=3, tiled=True)
    ctx_keys = ctx_kv[:, :, 0].reshape(images, ctx_len, heads_here, HEAD)
    ctx_vals = ctx_kv[:, :, 1].reshape(images, ctx_len, heads_here, HEAD)
    live = (jnp.arange(ctx_len)[None, :] < CLIPTOK + text_len[:, None])[:, None, None, :]

    def piece_scores(segment):
        length = segment.shape[0]
        seg_keys = segment[:, :, 0].reshape(length, images, heads_here, HEAD)
        seg_vals = segment[:, :, 1].reshape(length, images, heads_here, HEAD)
        scores = (
            jnp.einsum("iqhd,kihd->ihqk", query, seg_keys, preferred_element_type=jnp.float32)
            * score_scale
        )
        return (scores, seg_keys, seg_vals)

    ctx_scores = jnp.where(
        live,
        jnp.einsum("iqhd,ikhd->ihqk", query, ctx_keys, preferred_element_type=jnp.float32)
        * score_scale,
        -1e30,
    )
    kv_all = lax.all_gather(kv_local, "blk", axis=0, tiled=True)

    def stat_step(position, carry):
        top_val, total = carry
        segment = lax.dynamic_slice_in_dim(kv_all, position * key_block, key_block, 0)
        scores = piece_scores(segment)[0]
        new_top = jnp.maximum(top_val, jnp.max(scores, axis=-1))
        total = total * jnp.exp(top_val - new_top) + jnp.sum(
            jnp.exp(scores - new_top[..., None]), axis=-1
        )
        return (new_top, total)

    first_top = jnp.max(ctx_scores, axis=-1)
    first_total = jnp.sum(jnp.exp(ctx_scores - first_top[..., None]), axis=-1)
    row_max, row_total = lax.fori_loop(0, block_total, stat_step, (first_top, first_total))

    def weights_of(scores):
        return jnp.exp(scores - row_max[..., None]) / row_total[..., None]

    def out_step(position, accum):
        segment = lax.dynamic_slice_in_dim(kv_all, position * key_block, key_block, 0)
        scores, seg_keys, seg_vals = piece_scores(segment)
        return accum + jnp.einsum(
            "ihqk,kihd->iqhd",
            weights_of(scores).astype(jnp.bfloat16),
            seg_vals,
            preferred_element_type=jnp.float32,
        )

    attn_start = jnp.einsum(
        "ihqk,ikhd->iqhd",
        weights_of(ctx_scores).astype(jnp.bfloat16),
        ctx_vals,
        preferred_element_type=jnp.float32,
    )
    attn_f = lax.fori_loop(0, block_total, out_step, attn_start)
    attn_low = attn_f.reshape(images, pixels, local_width).astype(jnp.bfloat16)
    projected = lax.psum_scatter(
        jnp.einsum("ipc,cd->ipd", attn_low, out_weight, preferred_element_type=jnp.float32).astype(
            jnp.bfloat16
        ),
        "ch",
        scatter_dimension=2,
        tiled=True,
    ).astype(jnp.float32)
    block_output = (resid + projected.reshape(images, row_count, col_count, local_width)).astype(
        jnp.bfloat16
    )
    grad_all = lax.all_gather(cotangent, "ch", axis=3, tiled=True).reshape(images, pixels, channels)
    out_grad = jnp.einsum("ipc,ipd->cd", attn_low, grad_all, preferred_element_type=jnp.float32)
    d_attn = jnp.einsum(
        "ipd,cd->ipc", grad_all, out_weight, preferred_element_type=jnp.float32
    ).astype(jnp.bfloat16)
    d_attn4 = d_attn.reshape(images, pixels, heads_here, HEAD)
    delta = jnp.einsum("iqhd,iqhd->ihq", d_attn4.astype(jnp.float32), attn_f)
    ctx_probs = weights_of(ctx_scores)
    ctx_dprob = jnp.einsum("iqhd,ikhd->ihqk", d_attn4, ctx_vals, preferred_element_type=jnp.float32)
    ctx_dscore = (ctx_probs * (ctx_dprob - delta[..., None])).astype(jnp.bfloat16)
    d_ctx_keys = (
        jnp.einsum("ihqk,iqhd->ikhd", ctx_dscore, query, preferred_element_type=jnp.float32)
        * score_scale
    )
    d_ctx_vals = jnp.einsum(
        "ihqk,iqhd->ikhd",
        ctx_probs.astype(jnp.bfloat16),
        d_attn4,
        preferred_element_type=jnp.float32,
    )
    dq_start = (
        jnp.einsum("ihqk,ikhd->iqhd", ctx_dscore, ctx_keys, preferred_element_type=jnp.float32)
        * score_scale
    )

    def dq_step(position, accum):
        segment = lax.dynamic_slice_in_dim(kv_all, position * key_block, key_block, 0)
        scores, seg_keys, seg_vals = piece_scores(segment)
        dprob = jnp.einsum("iqhd,kihd->ihqk", d_attn4, seg_vals, preferred_element_type=jnp.float32)
        dscore = (weights_of(scores) * (dprob - delta[..., None])).astype(jnp.bfloat16)
        return (
            accum
            + jnp.einsum("ihqk,kihd->iqhd", dscore, seg_keys, preferred_element_type=jnp.float32)
            * score_scale
        )

    d_query = lax.fori_loop(0, block_total, dq_step, dq_start)
    segment = kv_all
    scores, seg_keys, seg_vals = piece_scores(segment)
    probs = weights_of(scores)
    dprob = jnp.einsum("iqhd,kihd->ihqk", d_attn4, seg_vals, preferred_element_type=jnp.float32)
    dscore = (probs * (dprob - delta[..., None])).astype(jnp.bfloat16)
    d_keys = (
        jnp.einsum("ihqk,iqhd->kihd", dscore, query, preferred_element_type=jnp.float32)
        * score_scale
    )
    d_vals = jnp.einsum(
        "ihqk,iqhd->kihd", probs.astype(jnp.bfloat16), d_attn4, preferred_element_type=jnp.float32
    )
    d_kv = lax.psum_scatter(
        jnp.stack(
            (
                d_keys.reshape(pixels * lax.axis_size("blk"), images, local_width),
                d_vals.reshape(pixels * lax.axis_size("blk"), images, local_width),
            ),
            axis=2,
        ),
        "blk",
        scatter_dimension=0,
        tiled=True,
    ).astype(jnp.bfloat16)
    d_qkv = jnp.concatenate(
        (
            d_query.reshape(images, pixels, 1, local_width).astype(jnp.bfloat16),
            jnp.transpose(d_kv, (1, 0, 2, 3)),
        ),
        axis=2,
    )
    qkv_grad = jnp.einsum("ipc,iptd->ctd", act_all, d_qkv, preferred_element_type=jnp.float32)
    d_act3 = lax.psum_scatter(
        jnp.einsum("iptd,ctd->ipc", d_qkv, qkv_weight, preferred_element_type=jnp.float32).astype(
            jnp.bfloat16
        ),
        "ch",
        scatter_dimension=2,
        tiled=True,
    ).astype(jnp.float32)
    d_act3 = d_act3.reshape(images, row_count, col_count, local_width)
    gain_three = jnp.sum(d_act3 * hat_three, axis=(0, 1, 2))
    bias_three = jnp.sum(d_act3, axis=(0, 1, 2))
    d_resid = cotangent.astype(jnp.float32) + norm_back(d_act3 * norm3_gain, hat_three, inv_three)
    saved = res_forward(input_f)
    hat_one, inv_one, pre_one, pad_one = (saved[0], saved[1], saved[2], saved[3])
    hat_two, inv_two, base_two, pre_two, pad_two = (
        saved[4],
        saved[5],
        saved[6],
        saved[7],
        saved[8],
    )
    conv2_grad, d_act2 = conv_back(pad_two, d_resid.astype(jnp.bfloat16), conv2_weight)
    d_pre2 = d_act2 * silu_slope(pre_two)
    d_scale_shift = jnp.stack(
        (jnp.sum(d_pre2 * base_two, axis=(1, 2)), jnp.sum(d_pre2, axis=(1, 2))), axis=1
    )
    embed_weight_grad = jnp.einsum(
        "ie,isc->esc", emb_act.astype(jnp.float32), d_scale_shift, precision=lax.Precision.HIGHEST
    )
    embed_bias_grad = jnp.sum(d_scale_shift, axis=0)
    d_base2 = d_pre2 * (1.0 + emb_scale)
    gain_two = jnp.sum(d_base2 * hat_two, axis=(0, 1, 2))
    bias_two = jnp.sum(d_base2, axis=(0, 1, 2))
    d_hidden1 = norm_back(d_base2 * norm2_gain, hat_two, inv_two).astype(jnp.bfloat16)
    conv1_grad, d_act1 = conv_back(pad_one, d_hidden1, conv1_weight)
    d_pre1 = d_act1 * silu_slope(pre_one)
    gain_one = jnp.sum(d_pre1 * hat_one, axis=(0, 1, 2))
    bias_one = jnp.sum(d_pre1, axis=(0, 1, 2))
    input_grad = d_resid + norm_back(d_pre1 * norm1_gain, hat_one, inv_one)
    ctx_partial = jnp.stack(
        (
            d_ctx_keys.reshape(images, ctx_len, local_width),
            d_ctx_vals.reshape(images, ctx_len, local_width),
        ),
        axis=2,
    )
    summed = lax.psum(
        (
            conv1_grad,
            conv2_grad,
            embed_weight_grad,
            embed_bias_grad,
            gain_one,
            bias_one,
            gain_two,
            bias_two,
            gain_three,
            bias_three,
            qkv_grad,
            out_grad,
            ctx_partial,
        ),
        "blk",
    )
    ctx_heads_all = lax.all_gather(summed[12].astype(jnp.bfloat16), "ch", axis=3, tiled=True)
    ctx_grad = jnp.einsum(
        "itx,itsc->xsc", context, ctx_heads_all, preferred_element_type=jnp.float32
    )
    return (
        block_output,
        input_grad,
        summed[0],
        summed[1],
        summed[2],
        summed[3],
        summed[4],
        summed[5],
        summed[6],
        summed[7],
        summed[8],
        summed[9],
        summed[10],
        summed[11],
        ctx_grad,
    )


def solution(mesh):
    return jax.shard_map(
        body,
        mesh=mesh,
        in_specs=(
            P(None, "blk", None, "ch"),
            P(None, "blk", None, "ch"),
            P(),
            P(),
            P(),
            P(None, None, "ch"),
            P(None, None, None, "ch"),
            P(None, None, None, "ch"),
            P(None, None, "ch"),
            P(None, "ch"),
            P("ch"),
            P("ch"),
            P("ch"),
            P("ch"),
            P("ch"),
            P("ch"),
            P(None, None, "ch"),
            P("ch", None),
            P("ch", None, None),
        ),
        out_specs=(
            P(None, "blk", None, "ch"),
            P(None, "blk", None, "ch"),
            P(None, None, None, "ch"),
            P(None, None, None, "ch"),
            P(None, None, "ch"),
            P(None, "ch"),
            P("ch"),
            P("ch"),
            P("ch"),
            P("ch"),
            P("ch"),
            P("ch"),
            P(None, None, "ch"),
            P("ch", None),
            P("ch", None, None),
        ),
        check_vma=False,
    )
```

profile of v0, /device:TPU:0, one launch (start us, length us, event | category | flops | bytes accessed | tf_op | source)
XLA Modules:
  0.0 833.7 jit_solution(4494627912396374353)
XLA Ops:
  8.8 15.1 %all-reduce.9 = (f32[2,8]{1,0:T(2,128)S(1)}, f32[2,8]{1,0:T(2,128)S(1)}) all-reduce(f32[2,8]{1,0:T(2,128)S(1)} %reduce_sum.354, f32[2,8]{1,0:T(2,128)S(1)} %reduce_sum.352), channel_id=1, replica_groups=mesh['blk'=8,'ch'=4] {'blk'}, use_global_device_ids=true, to_apply=%region_5.6 | all-reduce | flops 32 | bytes 256 | tf_op jit(solution)/shard_map/psum | solution.py:73
  28.6 27.2 %all-gather.7.cloned.1.call-done = bf16[2,8,64,512]{3,2,1,0:T(8,128)(2,1)} async-done(((bf16[2,8,64,128]{3,2,1,0:T(8,128)(2,1)}), bf16[2,8,64,512]{3,2,1,0:T(8,128)(2,1)}) %all-gather.7.cloned.1.call-update) | async-done | bytes 1048592 | tf_op jit(solution)/shard_map/all_gather | solution.py:95
  67.2 15.3 %all-reduce.8 = (f32[2,8]{1,0:T(2,128)S(1)}, f32[2,8]{1,0:T(2,128)S(1)}) all-reduce(f32[2,8]{1,0:T(2,128)S(1)} %reduce_sum.358, f32[2,8]{1,0:T(2,128)S(1)} %reduce_sum.356), channel_id=1, replica_groups=mesh['blk'=8,'ch'=4] {'blk'}, use_global_device_ids=true, to_apply=%region_11.12 | all-reduce | flops 32 | bytes 256 | tf_op jit(solution)/shard_map/psum | solution.py:73
  83.9 30.2 %all-gather.9.cloned.1.call-done = bf16[2,8,64,512]{3,2,1,0:T(8,128)(2,1)} async-done(((bf16[2,8,64,128]{3,2,1,0:T(8,128)(2,1)}), bf16[2,8,64,512]{3,2,1,0:T(8,128)(2,1)}) %all-gather.9.cloned.1.call-update) | async-done | bytes 1048592 | tf_op jit(solution)/shard_map/all_gather | solution.py:95
  125.9 15.3 %all-reduce.7 = (f32[2,8]{1,0:T(2,128)S(1)}, f32[2,8]{1,0:T(2,128)S(1)}) all-reduce(f32[2,8]{1,0:T(2,128)S(1)} %reduce_sum.362, f32[2,8]{1,0:T(2,128)S(1)} %reduce_sum.360), channel_id=1, replica_groups=mesh['blk'=8,'ch'=4] {'blk'}, use_global_device_ids=true, to_apply=%region_18.19 | all-reduce | flops 32 | bytes 256 | tf_op jit(solution)/shard_map/psum | solution.py:73
  142.8 2.8 convolution_convert_fusion
  145.6 4.1 copy.177
  151.6 21.1 %all-gather.11.cloned.1.call-done = bf16[2,8,64,512]{3,2,1,0:T(8,128)(2,1)} async-done(((bf16[2,8,64,128]{3,2,1,0:T(8,128)(2,1)}), bf16[2,8,64,512]{3,2,1,0:T(8,128)(2,1)}) %all-gather.11.cloned.1.call-update) | async-done | bytes 1048592 | tf_op jit(solution)/shard_map/all_gather | solution.py:95
  176.2 26.8 %reduce-scatter.19.cloned.1.call-done = bf16[128,1040]{1,0:T(8,128)(2,1)} async-done(((bf16[512,1040]{1,0:T(8,128)(2,1)}), bf16[128,1040]{1,0:T(8,128)(2,1)}) %reduce-scatter.19.cloned.1.call-update) | async-done | bytes 266256
  206.2 34.8 %all-gather.13.cloned.1.call-done = bf16[4096,2,2,128]{0,3,2,1:T(8,128)(2,1)} async-done(((bf16[512,2,2,128]{0,3,2,1:T(8,128)(2,1)}), bf16[4096,2,2,128]{0,3,2,1:T(8,128)(2,1)}) %all-gather.13.cloned.1.call-update) | async-done | bytes 4194320 | tf_op jit(solution)/shard_map/all_gather | solution.py:204
  240.9 4.7 copy.108
  245.7 20.2 %while.41 = (s32[]{:T(128)}, f32[2,2,512]{2,1,0:T(2,128)S(1)}, f32[2,2,512]{2,1,0:T(2,128)S(1)}, bf16[4096,2,2,128]{0,3,1,2:T(8,128)(2,1)}, bf16[2,512,2,64]{1,3...) while((s32[]{:T(128)}, f32[2,2,512]{2,1,0:T(2,128)S(1)}, ...), condition=%wide.region_24.25_spmd, body=%wide.region_21.24_spmd.sunk | while | flops 139464704 | bytes 9543823 | solution.py:218
  267.6 33.5 %while.42 = (s32[]{:T(128)}, f32[2,512,2,64]{1,3,2,0:T(8,128)}, bf16[4096,2,2,128]{0,3,1,2:T(8,128)(2,1)}, bf16[2,512,2,64]{1,3,2,0:T(8,128)(2,1)S(1)}, f32[2,2,...) while((s32[]{:T(128)}, f32[2,512,2,64]{1,3,2,0:T(8,128)}, ...), condition=%wide.region_26.27_spmd, body=%wide.region_25.26_spmd.sunk | while | flops 272760832 | bytes 2900143 | solution.py:239
  268.7 3.1 fusion.367
  272.9 3.1 fusion.367
  277.1 3.1 fusion.367
  281.2 3.1 fusion.367
  285.4 3.1 fusion.367
  289.6 3.1 fusion.367
  293.8 3.1 fusion.367
  298.0 3.1 fusion.367
  301.1 3.9 fusion.275
  305.0 12.6 %exponential_divide_fusion = f32[2,2,512,4096]{3,2,1,0:T(8,128)} fusion(f32[2,2,512]{2,1,0:T(2,128)S(1)} %get-tuple-element.933, f32[2,2,512]{2,1,0:T(2,128)S(1)} %get-tuple-element.917, bf16[2,512,2,64]{1,3,2,0:T(8,128)(2,1)S(1)} %get-tuple-element.885, bf16[4096,2,2,64]{0,3,2,1:T(8,128)(2,1)S(1)} %bitcast.583), kind=kOutput, calls=%fused_computation.22 | convolution fusion | flops 1098907648 | bytes 35930112 | tf_op jit(solution)/shard_map/iqhd,kihd->ihqk/dot_general | solution.py:193
  319.3 15.5 %fusion.12 = f32[2,2,64,4096]{3,2,1,0:T(8,128)} fusion(bf16[2,512,2,64]{1,3,2,0:T(8,128)(2,1)S(1)} %bitcast.574, f32[2,2,512,4096]{3,2,1,0:T(8,128)} %exponential_divide_fusion), kind=kOutput, calls=%fused_computation.24 | convolution fusion | flops 1082130432 | bytes 38010880 | tf_op jit(solution)/shard_map/ihqk,iqhd->kihd/dot_general | solution.py:298
  334.8 5.6 copy.113
  340.5 15.6 %fusion.17 = f32[2,2,64,4096]{3,2,1,0:T(8,128)} fusion(bf16[2,512,2,64]{1,3,2,0:T(8,128)(2,1)S(1)} %get-tuple-element.885, f32[2,2,512,4096]{3,2,1,0:T(8,128)} %exponential_divide_fusion, f32[2,2,512]{2,1,0:T(2,128)S(1)} %get-tuple-element.815, bf16[2,512,2,64]{1,3,2,0:T(8,128)(2,1)S(1)} %bitcast.575, bf16[4096,2,2,64]{0,3,2,1:T(8,128)(2,1)} %bitcast.562), kind=kOutput, calls=%fused_computation.29 | convolution fusion | flops 2173698048 | bytes 40378368 | tf_op jit(solution)/shard_map/ihqk,iqhd->kihd/dot_general | solution.py:295
  356.1 5.6 copy.112
  361.7 7.2 pad_maximum_fusion
  373.0 77.3 %while.43 = (s32[]{:T(128)}, f32[2,512,2,64]{1,3,2,0:T(8,128)}, bf16[4096,2,2,128]{0,3,1,2:T(8,128)(2,1)}, bf16[2,512,2,64]{1,3,2,0:T(8,128)(2,1)S(1)}, f32[2,2,...) while((s32[]{:T(128)}, f32[2,512,2,64]{1,3,2,0:T(8,128)}, ...), condition=%wide.region_29.30_spmd, body=%wide.region_28.29_spmd.sunk | while | flops 409206784 | bytes 11821247 | solution.py:288
  382.6 2.7 fusion.373
  385.3 4.8 fusion.374
  391.2 2.7 fusion.373
  394.0 4.9 fusion.374
  400.0 2.7 fusion.373
  402.7 5.0 fusion.374
  408.7 2.7 fusion.373
  411.4 4.7 fusion.374
  417.2 2.7 fusion.373
  419.9 4.7 fusion.374
  425.8 2.7 fusion.373
  428.5 4.7 fusion.374
  434.3 2.7 fusion.373
  437.0 4.8 fusion.374
  442.8 2.7 fusion.373
  445.6 4.7 fusion.374
  453.6 3.0 bitcast_convert_fusion
  456.6 3.7 copy.181
  462.8 27.6 %reduce-scatter.23.cloned.1.call-done = bf16[128,1024]{1,0:T(8,128)(2,1)} async-done(((bf16[512,1024]{1,0:T(8,128)(2,1)}), bf16[128,1024]{1,0:T(8,128)(2,1)}) %reduce-scatter.23.cloned.1.call-update) | async-done | bytes 262160
  493.5 13.4 %all-reduce.6 = (f32[2,8]{1,0:T(2,128)S(1)}, f32[2,8]{1,0:T(2,128)S(1)}) all-reduce(f32[2,8]{1,0:T(2,128)S(1)} %reduce_sum.367, f32[2,8]{1,0:T(2,128)S(1)} %reduce_sum.365), channel_id=1, replica_groups=mesh['blk'=8,'ch'=4] {'blk'}, use_global_device_ids=true, to_apply=%region_37.38 | all-reduce | flops 32 | bytes 256 | tf_op jit(solution)/shard_map/psum | solution.py:73
  509.8 3.0 collective-permute-start.4
  519.3 3.8 copy.183
  523.1 4.1 reshape.375
  527.3 26.6 %reduce-scatter.25.cloned.1.call-done = bf16[128,1024]{1,0:T(8,128)(2,1)} async-done(((bf16[512,1024]{1,0:T(8,128)(2,1)}), bf16[128,1024]{1,0:T(8,128)(2,1)}) %reduce-scatter.25.cloned.1.call-update) | async-done | bytes 262160
  558.2 2.9 multiply_reduce_fusion.1
  561.5 13.4 %all-reduce.5 = (f32[2,8]{1,0:T(2,128)S(1)}, f32[2,8]{1,0:T(2,128)S(1)}) all-reduce(f32[2,8]{1,0:T(2,128)S(1)} %reduce_sum.371, f32[2,8]{1,0:T(2,128)S(1)} %reduce_sum.369), channel_id=1, replica_groups=mesh['blk'=8,'ch'=4] {'blk'}, use_global_device_ids=true, to_apply=%region_44.45 | all-reduce | flops 32 | bytes 256 | tf_op jit(solution)/shard_map/psum | solution.py:73
  578.0 3.2 collective-permute-start.6
  587.7 3.8 copy.185
  591.5 4.1 reshape.377
  610.6 3.0 convolution_bitcast_fusion.1
  629.5 30.3 %all-reduce.15 = (f32[2,8]{1,0:T(2,128)S(1)}, f32[2,8]{1,0:T(2,128)S(1)}, f32[2,128]{1,0:T(2,128)}, f32[128]{0:T(128)}, f32[128]{0:T(128)}, /*index=5*/f32[128]{...) all-reduce(f32[2,8]{1,0:T(2,128)S(1)} %reduce_sum.375, ...), channel_id=1, replica_groups=mesh['blk'=8,'ch'=4] {'blk'}, use_global_device_ids=true, to_apply=%region_51.52 | all-reduce | flops 134176 | bytes 807168 | tf_op jit(solution)/shard_map/psum | solution.py:73
  661.4 2.6 fusion.48
  673.0 16.1 %all-gather.17.cloned.1.call-done = bf16[2,260,2,512]{3,1,0,2:T(8,128)(2,1)} async-done(((bf16[2,260,2,128]{3,1,0,2:T(8,128)(2,1)}), bf16[2,260,2,512]{3,1,0,2:T(8,128)(2,1)}) %all-gather.17.cloned.1.call-update) | async-done | bytes 1064976 | tf_op jit(solution)/shard_map/all_gather | solution.py:385
  693.9 121.4 %all-reduce.14.cloned.1.call-done = (f32[3,3,512,128]{3,2,1,0:T(8,128)}, f32[3,3,512,128]{3,2,1,0:T(8,128)}, f32[2048,2,128]{2,0,1:T(8,128)}, f32[512,3,128]{2,0,1:T(8,128)}, f32[128,512]{1,0:T(8,128)}) async-done(((f32[3,3,512,128]{3,2,1,0:T(8,128)}, f32[3,3,512,128]{3,2,1,0:T(8,128)}, f32[2048,2,128]{2,0,1:T(8,128)}, f32[512,3,128]{2,0,1:T(8,128)}, f32[128,512]{1,0:T(8,128)}), ...) | async-done | bytes 7864336 | tf_op jit(solution)/shard_map/psum | solution.py:367
  815.3 5.6 copy.120
  (468 shorter events, 168.9 us)
Async XLA Ops:
  7.2 20.5 %copy-start = (bf16[2048,2,128]{2,1,0:T(2,128)(2,1)S(1)}, bf16[2048,2,128]{2,1,0:T(2,128)(2,1)}, u32[]{:S(2)}) copy-start(bf16[2048,2,128]{2,1,0:T(2,128)(2,1)} %param.33) | copy-start | bytes 3145732
  7.2 52.3 %copy-start.26 = (bf16[3,3,512,128]{3,2,1,0:T(8,128)(2,1)S(1)}, bf16[3,3,512,128]{3,2,1,0:T(8,128)(2,1)}, u32[]{:S(2)}) copy-start(bf16[3,3,512,128]{3,2,1,0:T(8,128)(2,1)} %param.31) | copy-start | bytes 3538948
  7.2 48.6 %all-gather.7.cloned.1.call-start = ((), (), s32[]{:S(2)}) async-start(), calls=%async_computation.6 | async-start | bytes 1310720 | tf_op jit(solution)/shard_map/all_gather | solution.py:95
  24.2 37.0 %copy-start.56 = (f32[2,128]{1,0:T(2,128)}, f32[2,128]{1,0:T(2,128)S(1)}, u32[]{:S(2)}) copy-start(f32[2,128]{1,0:T(2,128)S(1)} %div.152) | copy-start | bytes 3076
  26.1 88.0 %all-gather.9.cloned.1.call-start = ((), (), s32[]{:S(2)}) async-start(), calls=%async_computation.7 | async-start | bytes 1310720 | tf_op jit(solution)/shard_map/all_gather | solution.py:95
  55.8 6.3 copy-start.4
  56.9 4.3 collective-permute-start
  58.2 3.9 collective-permute-start.1
  66.3 16.6 %copy-start.71 = (f32[128]{0:T(128)S(1)}, f32[128]{0:T(128)}, u32[]{:S(2)}) copy-start(f32[128]{0:T(128)} %param.37) | copy-start | bytes 1540
  66.3 16.6 %copy-start.74 = (f32[128]{0:T(128)S(1)}, f32[128]{0:T(128)}, u32[]{:S(2)}) copy-start(f32[128]{0:T(128)} %param.38) | copy-start | bytes 1540
  66.3 51.5 %copy-start.24 = (bf16[3,3,512,128]{3,2,1,0:T(8,128)(2,1)S(1)}, bf16[3,3,512,128]{3,2,1,0:T(8,128)(2,1)}, u32[]{:S(2)}) copy-start(bf16[3,3,512,128]{3,2,1,0:T(8,128)(2,1)} %param.32) | copy-start | bytes 3538948
  66.8 17.1 %copy-start.13 = (f32[2,8,64,128]{3,2,1,0:T(8,128)}, f32[2,8,64,128]{3,2,1,0:T(8,128)S(1)}, u32[]{:S(2)}) copy-start(f32[2,8,64,128]{3,2,1,0:T(8,128)S(1)} %get-tuple-element.611) | copy-start | bytes 1572868
  67.2 16.7 %copy-start.65 = (f32[2,128]{1,0:T(2,128)}, f32[2,128]{1,0:T(2,128)S(1)}, u32[]{:S(2)}) copy-start(f32[2,128]{1,0:T(2,128)S(1)} %get-tuple-element.609) | copy-start | bytes 3076
  67.2 16.7 %copy-start.69 = (f32[2,128]{1,0:T(2,128)}, f32[2,128]{1,0:T(2,128)S(1)}, u32[]{:S(2)}) copy-start(f32[2,128]{1,0:T(2,128)S(1)} %get-tuple-element.610) | copy-start | bytes 3076
  83.8 88.9 %all-gather.11.cloned.1.call-start = ((), (), s32[]{:S(2)}) async-start(), calls=%async_computation.8 | async-start | bytes 1310720 | tf_op jit(solution)/shard_map/all_gather | solution.py:95
  114.1 6.3 copy-start.6
  115.2 4.3 collective-permute-start.2
  116.5 3.9 collective-permute-start.3
  125.0 16.6 %copy-start.67 = (f32[128]{0:T(128)S(1)}, f32[128]{0:T(128)}, u32[]{:S(2)}) copy-start(f32[128]{0:T(128)} %param.39) | copy-start | bytes 1540
  125.0 16.6 %copy-start.81 = (f32[128]{0:T(128)S(1)}, f32[128]{0:T(128)}, u32[]{:S(2)}) copy-start(f32[128]{0:T(128)} %param.40) | copy-start | bytes 1540
  125.0 17.7 %copy-start.82 = (bf16[512,2,512]{2,1,0:T(2,128)(2,1)S(1)}, bf16[512,2,512]{2,1,0:T(2,128)(2,1)}, u32[]{:S(2)}) copy-start(bf16[512,2,512]{2,1,0:T(2,128)(2,1)} %param.43) | copy-start | bytes 3145732
  125.6 19.9 %copy-start.2 = (f32[2,8,64,128]{3,2,1,0:T(8,128)}, f32[2,8,64,128]{3,2,1,0:T(8,128)S(1)}, u32[]{:S(2)}) copy-start(f32[2,8,64,128]{3,2,1,0:T(8,128)S(1)} %get-tuple-element.612) | copy-start | bytes 1572868
  141.4 4.1 copy-start.48
  142.5 60.6 %reduce-scatter.19.cloned.1.call-start = ((), (), s32[]{:S(2)}) async-start(), calls=%async_computation.13 | async-start | bytes 1474560
  149.6 23.1 %copy-start.83 = (bf16[512,3,128]{2,0,1:T(8,128)(2,1)S(1)}, bf16[512,3,128]{2,0,1:T(8,128)(2,1)}, u32[]{:S(2)}) copy-start(bf16[512,3,128]{2,0,1:T(8,128)(2,1)} %param.41) | copy-start | bytes 1179652
  151.6 24.6 %copy-start.84 = (s32[2]{0:T(128)S(1)}, s32[2]{0:T(128)}, u32[]{:S(2)}) copy-start(s32[2]{0:T(128)} %param.29) | copy-start | bytes 28
  151.6 89.4 %all-gather.13.cloned.1.call-start = ((), (), s32[]{:S(2)}) async-start(), calls=%async_computation.9 | async-start | bytes 4718592 | tf_op jit(solution)/shard_map/all_gather | solution.py:204
  175.5 142.1 %all-gather.15.cloned.1.call-start = ((), (), s32[]{:S(2)}) async-start(), calls=%async_computation.10 | async-start | bytes 1310720 | tf_op jit(solution)/shard_map/all_gather | solution.py:252
  176.1 276.2 %reduce-scatter.17.cloned.1.call-start = ((), (), s32[]{:S(2)}) async-start(), calls=%async_computation.11 | async-start | bytes 9437184 | tf_op jit(solution)/shard_map/reduce_scatter | solution.py:301
  205.0 60.9 %copy-start.46 = (bf16[2,260,1,128]{1,3,0,2:T(8,128)(2,1)}, bf16[2,260,1,128]{1,3,0,2:T(8,128)(2,1)S(1)}, u32[]{:S(2)}) copy-start(bf16[2,260,1,128]{1,3,0,2:T(8,128)(2,1)S(1)} %copy.188) | copy-start | bytes 399364
  305.0 12.6 %copy-start.36 = (f32[2,512,2,64]{1,3,2,0:T(8,128)S(1)}, f32[2,512,2,64]{1,3,2,0:T(8,128)}, u32[]{:S(2)}) copy-start(f32[2,512,2,64]{1,3,2,0:T(8,128)} %get-tuple-element.360) | copy-start | bytes 1572868
  369.0 121.5 %reduce-scatter.23.cloned.1.call-start = ((), (), s32[]{:S(2)}) async-start(), calls=%async_computation.15 | async-start | bytes 1310720
  450.2 6.3 copy-start.28
  453.6 6.6 copy-start.42
  460.2 31.6 %copy-start.68 = (f32[128]{0:T(128)S(1)}, f32[128]{0:T(128)}, u32[]{:S(2)}) copy-start(f32[128]{0:T(128)} %param.39) | copy-start | bytes 1540
  460.2 32.3 %copy-start.3 = (f32[2,8,64,128]{3,2,1,0:T(8,128)S(1)}, f32[2,8,64,128]{3,2,1,0:T(8,128)}, u32[]{:S(2)}) copy-start(f32[2,8,64,128]{3,2,1,0:T(8,128)} %copy-done.2) | copy-start | bytes 1572868
  460.2 32.3 %copy-start.49 = (f32[2,128]{1,0:T(2,128)S(1)}, f32[2,128]{1,0:T(2,128)}, u32[]{:S(2)}) copy-start(f32[2,128]{1,0:T(2,128)} %copy-done.48) | copy-start | bytes 3076
  460.2 32.3 %copy-start.55 = (f32[2,128]{1,0:T(2,128)S(1)}, f32[2,128]{1,0:T(2,128)}, u32[]{:S(2)}) copy-start(f32[2,128]{1,0:T(2,128)} %copy-done.54) | copy-start | bytes 3076
  462.8 91.2 %reduce-scatter.25.cloned.1.call-start = ((), (), s32[]{:S(2)}) async-start(), calls=%async_computation.16 | async-start | bytes 1310720
  507.3 7.1 copy-start.25
  508.5 5.7 collective-permute-start.5
  509.8 4.4 collective-permute-start.4
  527.2 31.0 %copy-start.59 = (f32[2,128]{1,0:T(2,128)S(1)}, f32[2,128]{1,0:T(2,128)}, u32[]{:S(2)}) copy-start(f32[2,128]{1,0:T(2,128)} %copy-done.58) | copy-start | bytes 3076
  527.2 31.0 %copy-start.64 = (f32[2,128]{1,0:T(2,128)S(1)}, f32[2,128]{1,0:T(2,128)}, u32[]{:S(2)}) copy-start(f32[2,128]{1,0:T(2,128)} %copy-done.63) | copy-start | bytes 3076
  527.2 31.0 %copy-start.66 = (f32[2,128]{1,0:T(2,128)S(1)}, f32[2,128]{1,0:T(2,128)}, u32[]{:S(2)}) copy-start(f32[2,128]{1,0:T(2,128)} %copy-done.65) | copy-start | bytes 3076
  527.2 31.0 %copy-start.70 = (f32[2,128]{1,0:T(2,128)S(1)}, f32[2,128]{1,0:T(2,128)}, u32[]{:S(2)}) copy-start(f32[2,128]{1,0:T(2,128)} %copy-done.69) | copy-start | bytes 3076
  527.2 31.0 %copy-start.72 = (f32[128]{0:T(128)S(1)}, f32[128]{0:T(128)}, u32[]{:S(2)}) copy-start(f32[128]{0:T(128)} %param.37) | copy-start | bytes 1540
  527.2 31.0 %copy-start.75 = (f32[128]{0:T(128)S(1)}, f32[128]{0:T(128)}, u32[]{:S(2)}) copy-start(f32[128]{0:T(128)} %param.38) | copy-start | bytes 1540
  527.3 98.0 %reduce-scatter.27.cloned.1.call-start = ((), (), s32[]{:S(2)}) async-start(), calls=%async_computation.17 | async-start | bytes 1310720
  575.2 7.5 copy-start.27
  576.7 8.7 %copy-start.14 = (bf16[2,8,64,128]{3,2,1,0:T(8,128)(2,1)}, bf16[2,8,64,128]{3,2,1,0:T(8,128)(2,1)S(1)}, u32[]{:S(2)}) copy-start(bf16[2,8,64,128]{3,2,1,0:T(8,128)(2,1)S(1)} %multiply_convert_fusion.6) | copy-start | bytes 786436
  576.7 5.9 collective-permute-start.7
  578.0 4.6 collective-permute-start.6
  595.6 74.4 %reduce-scatter.21.cloned.1.call-start = ((), (), s32[]{:S(2)}) async-start(), calls=%async_computation.14 | async-start | bytes 1310720
  599.9 4.0 copy-start.44
  610.3 78.8 %all-gather.17.cloned.1.call-start = ((), (), s32[]{:S(2)}) async-start(), calls=%async_computation.12 | async-start | bytes 1351680 | tf_op jit(solution)/shard_map/all_gather | solution.py:385
  624.0 5.5 copy-start.35
  624.0 5.5 copy-start.76
  624.0 5.5 copy-start.77
  624.0 5.5 copy-start.79
  624.0 5.5 copy-start.80
  625.2 35.0 %copy-start.5 = (bf16[2,8,64,512]{3,2,1,0:T(8,128)(2,1)S(1)}, bf16[2,8,64,512]{3,2,1,0:T(8,128)(2,1)}, u32[]{:S(2)}) copy-start(bf16[2,8,64,512]{3,2,1,0:T(8,128)(2,1)} %all-gather.7.cloned.1.call-done) | copy-start | bytes 3145732
  659.9 155.4 %all-reduce.14.cloned.1.call-start = ((), (), s32[]{:S(2)}) async-start(), calls=%async_computation.18 | async-start | bytes 15728640 | tf_op jit(solution)/shard_map/psum | solution.py:367
  815.3 5.6 copy-start.30
  (42 other events, 94.5 us)
Sparse Core Ops, SparseCore 0:
  26.2 29.5 all-gather.6
  84.0 30.1 all-gather.8
  142.6 30.1 all-gather.10
  175.5 27.4 reduce-scatter.18
  204.8 36.1 all-gather.12
  242.4 30.1 all-gather.14
  369.1 71.2 reduce-scatter.16
  462.9 27.4 reduce-scatter.22
  527.4 26.4 reduce-scatter.24
  595.8 26.2 reduce-scatter.26
  625.0 25.7 reduce-scatter.20
  660.0 29.0 all-gather.16
  694.6 120.6 all-reduce.13
where the time goes:
time: 845 us; the launch traced here: 834 us
  waiting for transfers between devices  334 us (40%)
  matrix products  203 us (24%)
  local copies, waits for them, and re-layouts  116 us (14%)
  blocking collectives  103 us (12%)
  other arithmetic  36.9 us (4%)
  between operations  15.7 us (2%)
  starting transfers between devices  15.4 us (2%)
  loops' own time  8.86 us (1%)
    psum x1, waiting for transfers between devices, body(): lax.psum((conv1_grad, conv2_grad, embed_weight_grad, embed_bias_grad, gai...  121 us
    psum x6, blocking collectives, group_means(): total_first, total_second = lax.psum((first_g, second_g), 'blk')  103 us
    unnamed x18, waiting for transfers between devices  81.8 us
    all_gather x3, waiting for transfers between devices, all_channels(): return lax.all_gather(field, 'ch', axis=3, tiled=True)  78.5 us
    unnamed x199, local copies, waits for them, and re-layouts  62.1 us
    dot_general x17, matrix products, piece_scores(): jnp.einsum('iqhd,kihd->ihqk', query, seg_keys, preferred_element_type=jnp...  40.5 us
    dot_general x8, matrix products, dq_step(): jnp.einsum('ihqk,kihd->iqhd', dscore, seg_keys, preferred_element_type=jn...  38.3 us
    all_gather x1, waiting for transfers between devices, body(): kv_all = lax.all_gather(kv_local, 'blk', axis=0, tiled=True)  34.8 us
  transfers between devices with their start and end apart: 21, of which 11 were waited for; matrix products, arithmetic and copies ran while one was open for 26% of the time, Pallas kernels for 0%

commit v1 on v0

v1 whole, which is shorter than its diff:
```python
import functools
import math

import jax
import jax.numpy as jnp
from jax import lax
from jax.experimental import pallas as pl
from jax.experimental.pallas import tpu as pltpu
from jax.sharding import PartitionSpec as P

HEAD = 64
GROUPS = 32
CLIPTOK = 4
LANES = 128
HALF = 256
COLS = 64
VMEM_BYTES = 56 * 2**20
BF = jnp.bfloat16
F32 = jnp.float32


def dot(a, b):
    return jnp.dot(a, b, preferred_element_type=F32)


def dot_t(a, b):
    return lax.dot_general(a, b, (((1,), (1,)), ((), ())), preferred_element_type=F32)


def group_sum(vec, size):
    lane = lax.broadcasted_iota(jnp.int32, vec.shape, 1)
    step = 1
    while step < size:
        low = pltpu.roll(vec, step, 1)
        high = pltpu.roll(vec, LANES - step, 1)
        vec = vec + jnp.where((lane & step) != 0, low, high)
        step *= 2
    return vec


def norm_stats(sums, cells, size):
    total = group_sum(sums, size)
    mean = total[0:1] / cells
    inv = lax.rsqrt(total[1:2] / cells - mean * mean + 1e-05)
    return mean, inv


def affine_of(vec, shard, which, mean, inv):
    row = vec[pl.ds(shard, 1)][0]
    gain = row[2 * which : 2 * which + 1]
    bias = row[2 * which + 1 : 2 * which + 2]
    if which == 1:
        grow = 1.0 + row[6:7]
        gain, bias = gain * grow, bias * grow + row[7:8]
    slope = inv * gain
    return gain, slope, bias - mean * slope


def shards(scal):
    h = scal[0]
    return (h, h + 2, 1 - h, 3 - h)


def lanes_of(shard):
    return pl.ds(pl.multiple_of(shard * LANES, LANES), LANES)


def column_sums(first, second):
    rows = jnp.concatenate(
        [jnp.sum(first, axis=0, keepdims=True), jnp.sum(second, axis=0, keepdims=True)], axis=0
    )
    return jnp.concatenate([rows, jnp.zeros((6, rows.shape[1]), F32)], axis=0)


def shift_columns(total, left, right):
    col = lax.broadcasted_iota(jnp.int32, total.shape, 0) % COLS
    rows = total.shape[0]
    total = total + jnp.where(col > 0, pltpu.roll(left, 1, 0), 0.0)
    return total + jnp.where(col < COLS - 1, pltpu.roll(right, rows - 1, 0), 0.0)


def load_weights(scal, own_w, oth_w, w_scr):
    i = scal[1]
    w_scr[:, lanes_of(i)] = own_w[...]
    w_scr[:, lanes_of(1 - i)] = oth_w[...]


def conv_kernel(scal, own, oth, top, bot, sums, vec, own_w, oth_w, *rest, which, cells, size):
    if which == 0:
        out_low, out_sums, act_out, act_scr, w_scr = rest
    else:
        base, out_f, out_low, out_sums, act_out, act_scr, w_scr = rest
    pix = own.shape[0]
    load_weights(scal, own_w, oth_w, w_scr)
    for quarter, shard in enumerate(shards(scal)):
        lanes = slice(quarter * LANES, (quarter + 1) * LANES)
        mean, inv = norm_stats(sums[:, lanes], cells, size)
        gain, slope, offset = affine_of(vec, shard, which, mean, inv)

        def active(field):
            pre = field.astype(F32) * slope + offset
            return pre * jax.nn.sigmoid(pre)

        half = own if quarter < 2 else oth
        main = active(half[:, (quarter % 2) * LANES : (quarter % 2 + 1) * LANES])
        act_scr[COLS : COLS + pix, lanes_of(shard)] = main.astype(BF)
        act_scr[0:COLS, lanes_of(shard)] = jnp.where(
            scal[2] > 0, active(top[:, lanes]), 0.0
        ).astype(BF)
        act_scr[COLS + pix :, lanes_of(shard)] = jnp.where(
            scal[3] > 0, active(bot[:, lanes]), 0.0
        ).astype(BF)
    act_out[...] = act_scr[COLS : COLS + pix, :]
    channels = act_scr.shape[1]
    parts = []
    for kx in range(3):
        acc = None
        for ky in range(3):
            tap = (ky * 3 + kx) * channels
            term = dot(act_scr[ky * COLS : ky * COLS + pix, :], w_scr[tap : tap + channels, :])
            acc = term if acc is None else acc + term
        parts.append(acc)
    result = shift_columns(parts[1], parts[0], parts[2])
    if which == 1:
        result = result + base[...].astype(F32)
        out_f[...] = result
    out_low[...] = result.astype(BF)
    out_sums[...] = column_sums(result, result * result)


def qkv_kernel(
    scal, own, oth, sums, vec, cot_own, cot_oth, own_w, oth_w, out, act_out, cot_out, *, cells, size
):
    i = scal[1]
    for quarter, shard in enumerate(shards(scal)):
        lanes = slice(quarter * LANES, (quarter + 1) * LANES)
        part = slice((quarter % 2) * LANES, (quarter % 2 + 1) * LANES)
        mean, inv = norm_stats(sums[:, lanes], cells, size)
        gain, slope, offset = affine_of(vec, shard, 2, mean, inv)
        half = own if quarter < 2 else oth
        cot = cot_own if quarter < 2 else cot_oth
        act_out[:, lanes_of(shard)] = (half[:, part].astype(F32) * slope + offset).astype(BF)
        cot_out[:, lanes_of(shard)] = cot[:, part]
    for weight, first in ((own_w, 2 * i), (oth_w, 2 - 2 * i)):
        for head in range(2):
            columns = weight[:, head * HALF : (head + 1) * HALF]
            fwd = dot(act_out[...], columns)
            back = dot(cot_out[...], columns)
            lane = lax.broadcasted_iota(jnp.int32, fwd.shape, 1)
            out[pl.ds(first + head, 1)] = jnp.where(lane < 3 * HEAD, fwd, back).astype(BF)[None]


def below_stats(scal, total, own, oth, sums, vec, out_own, out_oth, out_stats, which, cells, size):
    for quarter, shard in enumerate(shards(scal)):
        lanes = slice(quarter * LANES, (quarter + 1) * LANES)
        part = slice((quarter % 2) * LANES, (quarter % 2 + 1) * LANES)
        mean, inv = norm_stats(sums[:, lanes], cells, size)
        gain, slope, offset = affine_of(vec, shard, which, mean, inv)
        half = own if quarter < 2 else oth
        grad = total[:, lanes_of(shard)]
        if quarter < 2:
            out_own[:, part] = grad
        else:
            out_oth[:, part] = grad.astype(BF)
        field = half[:, part].astype(F32)
        if which < 2:
            grad = grad * silu_slope(field * slope + offset)
        out_stats[:, lanes] = column_sums(grad, grad * ((field - mean) * inv))


def silu_slope(field):
    sigma = jax.nn.sigmoid(field)
    return sigma * (1.0 + field * (1.0 - sigma))


def qkv_back_kernel(
    scal, grads, own_w, oth_w, own, oth, sums, vec, out_own, out_oth, out_stats, tot_scr, *, cells, size
):
    i = scal[1]
    total = None
    for weight, first in ((own_w, 2 * i), (oth_w, 2 - 2 * i)):
        for head in range(2):
            columns = weight[:, head * HALF : (head + 1) * HALF]
            grad = grads[pl.ds(first + head, 1)][0]
            lane = lax.broadcasted_iota(jnp.int32, grad.shape, 1)
            term = dot_t(jnp.where(lane < 3 * HEAD, grad, jnp.zeros_like(grad)), columns)
            total = term if total is None else total + term
    tot_scr[...] = total
    below_stats(scal, tot_scr, own, oth, sums, vec, out_own, out_oth, out_stats, 2, cells, size)


def out_kernel(scal, grads, own_w, oth_w, act, cot, proj_own, proj_oth, keep, send, tot_scr):
    i = scal[1]
    total = None
    act_t = act[...].astype(F32).T.astype(BF)
    cot_t = cot[...].astype(F32).T.astype(BF)
    for weight, first, result in ((own_w, 2 * i, keep), (oth_w, 2 - 2 * i, send)):
        for head in range(2):
            lanes = slice(head * HALF, (head + 1) * HALF)
            columns = weight[:, lanes]
            grad = grads[pl.ds(first + head, 1)][0]
            lane = lax.broadcasted_iota(jnp.int32, grad.shape, 1)
            term = dot_t(jnp.where(lane < 3 * HEAD, jnp.zeros_like(grad), grad), columns)
            total = term if total is None else total + term
            first_grad, second_grad = dot(act_t, grad), dot(cot_t, grad)
            lane = lax.broadcasted_iota(jnp.int32, first_grad.shape, 1)
            result[:, lanes] = jnp.where(lane < 3 * HEAD, first_grad, second_grad).astype(
                result.dtype
            )
    tot_scr[...] = total
    for quarter, shard in enumerate(shards(scal)):
        part = slice((quarter % 2) * LANES, (quarter % 2 + 1) * LANES)
        if quarter < 2:
            proj_own[:, part] = tot_scr[:, lanes_of(shard)]
        else:
            proj_oth[:, part] = tot_scr[:, lanes_of(shard)].astype(BF)


def norm_back(scal, quarter, shard, sums, vec, stats, which, cells, size):
    lanes = slice(quarter * LANES, (quarter + 1) * LANES)
    mean, inv = norm_stats(sums[:, lanes], cells, size)
    gain, slope, offset = affine_of(vec, shard, which, mean, inv)
    means = group_sum(stats[:, lanes] * gain, size) / cells

    def back(grad, field):
        field = field.astype(F32)
        hat = (field - mean) * inv
        if which < 2:
            grad = grad * silu_slope(field * slope + offset)
        return (grad * gain - means[0:1] - hat * means[1:2]) * inv

    return back


def conv_back_kernel(
    scal, part_own, part_recv, dtop, dbot, field, ftop, fbot, sums, stats, vec,
    own_w, oth_w, low_own, low_oth, low_sums, *rest, which, cells, size,
):
    if which == 2:
        cot, ctop, cbot, out_f, ext, out_own, out_oth, out_stats, w_scr, tot_scr = rest
    else:
        ext, out_own, out_oth, out_stats, w_scr, tot_scr = rest
    pix = part_own.shape[0]
    load_weights(scal, own_w, oth_w, w_scr)
    for quarter in range(2):
        shard = shards(scal)[quarter]
        lanes = slice(quarter * LANES, (quarter + 1) * LANES)
        back = norm_back(scal, quarter, shard, sums, vec, stats, which, cells, size)
        main = back(part_own[:, lanes] + part_recv[:, lanes].astype(F32), field[:, lanes])
        head = back(dtop[:, lanes].astype(F32), ftop[:, lanes])
        tail = back(dbot[:, lanes].astype(F32), fbot[:, lanes])
        if which == 2:
            main = main + cot[:, lanes].astype(F32)
            head = head + ctop[:, lanes].astype(F32)
            tail = tail + cbot[:, lanes].astype(F32)
            out_f[:, lanes] = main
        ext[COLS : COLS + pix, lanes] = main.astype(BF)
        ext[0:COLS, lanes] = jnp.where(scal[2] > 0, head, 0.0).astype(BF)
        ext[COLS + pix :, lanes] = jnp.where(scal[3] > 0, tail, 0.0).astype(BF)
    channels = tot_scr.shape[1]
    parts = []
    for kx in range(3):
        acc = None
        for ky in range(3):
            tap = (ky * 3 + kx) * channels
            rows = (2 - ky) * COLS
            term = dot_t(ext[rows : rows + pix, :], w_scr[tap : tap + channels, :])
            acc = term if acc is None else acc + term
        parts.append(acc)
    tot_scr[...] = shift_columns(parts[1], parts[2], parts[0])
    below_stats(
        scal, tot_scr, low_own, low_oth, low_sums, vec, out_own, out_oth, out_stats,
        which - 1, cells, size,
    )


def last_kernel(
    scal, part_own, part_recv, field, sums, stats, vec, resid_grad, keep, send, tot_scr, *, cells, size
):
    i = scal[1]
    for quarter in range(2):
        shard = shards(scal)[quarter]
        lanes = slice(quarter * LANES, (quarter + 1) * LANES)
        back = norm_back(scal, quarter, shard, sums, vec, stats, 0, cells, size)
        main = back(part_own[:, lanes] + part_recv[:, lanes].astype(F32), field[:, lanes])
        tot_scr[:, lanes] = main + resid_grad[:, lanes]
    keep[...] = tot_scr[:, lanes_of(i)]
    send[...] = tot_scr[:, lanes_of(1 - i)].astype(BF)


def weight_grad_kernel(act_one, act_two, ext_one, ext_two, out, rhs_scr):
    pix, channels = act_one.shape
    rows = ext_one.shape[0]
    total = None
    for act, ext in ((act_one, ext_one), (act_two, ext_two)):
        wide = ext[...].astype(F32)
        col = lax.broadcasted_iota(jnp.int32, wide.shape, 0) % COLS
        for kx in range(3):
            if kx == 0:
                moved = jnp.where(col < COLS - 1, pltpu.roll(wide, rows - 1, 0), 0.0)
            elif kx == 2:
                moved = jnp.where(col > 0, pltpu.roll(wide, 1, 0), 0.0)
            else:
                moved = wide
            moved = moved.astype(BF)
            for ky in range(3):
                start = (2 - ky) * COLS
                tap = ky * 3 + kx
                rhs_scr[:, tap * LANES : (tap + 1) * LANES] = moved[start : start + pix]
        act_t = act[...].astype(F32).T.astype(BF)
        for tap in range(9):
            term = dot(act_t, rhs_scr[:, tap * LANES : (tap + 1) * LANES])
            if act is act_one:
                out[tap * channels : (tap + 1) * channels, :] = term
            else:
                out[tap * channels : (tap + 1) * channels, :] += term


def attend_kernel(
    live, qd, kva, kvb, ctx, dqo, dkva, dkvb, dctx,
    kv_scr, kt_scr, vt_scr, s_scr, e_scr, acc_scr, *, chunk, unroll,
):
    step = pl.program_id(0)
    half_a, half_b, extra = kva.shape[0], kvb.shape[0], ctx.shape[0]
    keys = half_a + half_b
    total = keys + extra
    block = qd.shape[0]

    @pl.when(step == 0)
    def _():
        kv_scr[0:half_a, :] = kva[...]
        kv_scr[half_a:keys, :] = kvb[...]
        kv_scr[keys:total, :] = ctx[...]
        acc_scr[...] = jnp.zeros_like(acc_scr)

        def turn(rows):
            flipped = kv_scr[rows, :].astype(F32).T.astype(BF)
            kt_scr[:, rows] = flipped[:HEAD]
            vt_scr[0:HEAD, rows] = flipped[HEAD:]

        def turn_step(n, carry):
            turn(pl.ds(pl.multiple_of(n * 256, 256), 256))
            return carry

        lax.fori_loop(0, keys // 256, turn_step, 0)
        turn(slice(keys, total))
        vt_scr[HEAD:, :] = jnp.ones((16, total), BF)

    both = qd[...].astype(F32).T
    q_t = both[:HEAD].astype(BF)
    zero = jnp.zeros((HEAD, block), BF)
    q_side = jnp.concatenate([q_t, zero], axis=0)

    def score(rows, top, masked):
        s = dot(kv_scr[rows, :], q_side)
        if masked:
            index = lax.broadcasted_iota(jnp.int32, s.shape, 0)
            s = jnp.where(index < live[0], s, -1e30)
        s_scr[rows, :] = s
        return jnp.maximum(top, jnp.max(s.reshape(-1, 8, block), axis=0))

    def span(n):
        return pl.ds(pl.multiple_of(n * chunk, chunk), chunk)

    def over_keys(func, carry):
        return lax.fori_loop(
            0, keys // chunk, lambda n, c: func(span(n), c), carry, unroll=unroll
        )

    tail = pl.ds(keys, extra)
    top = score(tail, jnp.full((8, block), -1e30, F32), True)
    top = over_keys(lambda rows, c: score(rows, c, False), top)
    top = jnp.max(top, axis=0, keepdims=True)

    def weigh(rows, acc):
        e = jnp.exp(s_scr[rows, :] - top).astype(BF)
        e_scr[rows, :] = e
        return acc + dot(vt_scr[:, rows], e)

    out_t = weigh(tail, jnp.zeros((HEAD + 16, block), F32))
    out_t = over_keys(weigh, out_t)
    inv = 1.0 / out_t[HEAD : HEAD + 1]
    out_t = out_t[:HEAD] * inv
    d_t = both[HEAD:]
    delta = jnp.sum(d_t * out_t, axis=0, keepdims=True) * inv
    d_t = d_t * inv
    d_side = jnp.concatenate([zero, d_t.astype(BF)], axis=0)
    zero_q = jnp.zeros((block, HEAD), BF)
    rows_q = jnp.concatenate([qd[:, :HEAD], zero_q], axis=1)
    rows_d = jnp.concatenate([zero_q, d_t.T.astype(BF)], axis=1)
    right = jnp.concatenate([rows_q, rows_d], axis=0)

    def back(rows, acc):
        d_prob = dot(kv_scr[rows, :], d_side)
        e = e_scr[rows, :]
        d_score = (e.astype(F32) * (d_prob - delta)).astype(BF)
        acc_scr[rows, :] += dot(jnp.concatenate([d_score, e], axis=1), right)
        return acc + dot(kt_scr[:, rows], d_score)

    dq_t = back(tail, jnp.zeros((HEAD, block), F32))
    dq_t = over_keys(back, dq_t)
    dqo[...] = jnp.concatenate([dq_t, out_t], axis=0).T.astype(BF)

    @pl.when(step == pl.num_programs(0) - 1)
    def _():
        dkva[...] = acc_scr[0:half_a, :]
        dkvb[...] = acc_scr[half_a:keys, :].astype(BF)
        dctx[...] = acc_scr[keys:total, :]


def attend(live, recv, kva, kvb, ctx):
    queries = recv.shape[0]
    block = min(512, queries)
    half_a, half_b, extra = recv.shape[0] if kva is recv else kva.shape[0], kvb.shape[0], ctx.shape[0]
    total = half_a + half_b + extra
    whole = lambda shape: pl.BlockSpec(shape, lambda n: (0, 0))
    flops = 12 * queries * total * HEAD
    return pl.pallas_call(
        functools.partial(attend_kernel, chunk=512, unroll=4),
        grid=(queries // block,),
        in_specs=[
            pl.BlockSpec(memory_space=pltpu.SMEM),
            pl.BlockSpec((block, LANES), lambda n: (n, 1)),
            whole((half_a, LANES)),
            whole((half_b, LANES)),
            whole((extra, LANES)),
        ],
        out_specs=[
            pl.BlockSpec((block, LANES), lambda n: (n, 0)),
            whole((half_a, LANES)),
            whole((half_b, LANES)),
            whole((extra, LANES)),
        ],
        out_shape=[
            jax.ShapeDtypeStruct((queries, LANES), BF),
            jax.ShapeDtypeStruct((half_a, LANES), F32),
            jax.ShapeDtypeStruct((half_b, LANES), BF),
            jax.ShapeDtypeStruct((extra, LANES), F32),
        ],
        scratch_shapes=[
            pltpu.VMEM((total, LANES), BF),
            pltpu.VMEM((HEAD, total), BF),
            pltpu.VMEM((HEAD + 16, total), BF),
            pltpu.VMEM((total, block), F32),
            pltpu.VMEM((total, block), BF),
            pltpu.VMEM((total, LANES), F32),
        ],
        compiler_params=pltpu.CompilerParams(vmem_limit_bytes=VMEM_BYTES),
        cost_estimate=pl.CostEstimate(
            flops=4 * flops, bytes_accessed=8 * total * LANES, transcendentals=queries * total
        ),
    )(live, recv, kva, kvb, ctx)


def call(kernel, args, outs, scratch=(), flops=0, scalars=1):
    in_vmem = pl.BlockSpec(memory_space=pltpu.VMEM)
    in_smem = pl.BlockSpec(memory_space=pltpu.SMEM)
    size = sum(math.prod(a.shape) * a.dtype.itemsize for a in args)
    size += sum(math.prod(s) * jnp.dtype(d).itemsize for s, d in outs)
    return pl.pallas_call(
        kernel,
        in_specs=[in_smem] * scalars + [in_vmem] * (len(args) - scalars),
        out_specs=[in_vmem] * len(outs),
        out_shape=[jax.ShapeDtypeStruct(s, d) for s, d in outs],
        scratch_shapes=[pltpu.VMEM(s, d) for s, d in scratch],
        compiler_params=pltpu.CompilerParams(vmem_limit_bytes=VMEM_BYTES),
        cost_estimate=pl.CostEstimate(flops=flops, bytes_accessed=size, transcendentals=0),
    )(*args)


def embed_features(timesteps, image_embed):
    half_width = image_embed.shape[1] // 2
    freqs = jnp.exp(-math.log(10000.0) * jnp.arange(half_width, dtype=F32) / half_width)
    angles = timesteps.astype(F32)[:, None] * freqs[None, :]
    return jax.nn.silu(jnp.concatenate([jnp.cos(angles), jnp.sin(angles)], axis=1) + image_embed)


def body(
    block_input,
    cotangent,
    image_embed,
    timesteps,
    text_len,
    context,
    conv1_weight,
    conv2_weight,
    embed_weight,
    embed_bias,
    norm1_gain,
    norm1_bias,
    norm2_gain,
    norm2_bias,
    norm3_gain,
    norm3_bias,
    qkv_weight,
    out_weight,
    ctx_weight,
):
    images, row_count, col_count, width = block_input.shape
    channels = qkv_weight.shape[0]
    size = channels // GROUPS
    blocks = lax.axis_size("blk")
    pix = row_count * col_count
    cells = float(pix * blocks * size)
    split = blocks // 4
    ctx_len = context.shape[1]
    b = lax.axis_index("blk")
    z = lax.axis_index("ch")
    h, i = z % 2, z // 2
    scal = jnp.stack(
        [h, i, (b > 0).astype(jnp.int32), (b < blocks - 1).astype(jnp.int32)]
    ).astype(jnp.int32)

    def over_ch(value, mask):
        return lax.ppermute(value, "ch", [(n, n ^ mask) for n in range(4)])

    def over_blk(value, mask):
        return lax.ppermute(value, "blk", [(n, n ^ mask) for n in range(blocks)])

    def halo(first, last):
        up = [(n, n + 1) for n in range(blocks - 1)]
        down = [(n + 1, n) for n in range(blocks - 1)]
        return lax.ppermute(last, "blk", up), lax.ppermute(first, "blk", down)

    def halo_rows(field):
        return halo(field[:COLS], field[pix - COLS :])

    def blk_sum(value):
        spread = jnp.broadcast_to(value[None], (blocks,) + value.shape)
        return jnp.sum(lax.all_to_all(spread, "blk", 0, 0), axis=0)

    def by_image(first, second):
        return jnp.where(i == 0, first, second), jnp.where(i == 0, second, first)

    def halves(field):
        flat = field.reshape(images, pix, width)
        mine = lax.dynamic_index_in_dim(flat, i, 0, keepdims=False)
        theirs = lax.dynamic_index_in_dim(flat, 1 - i, 0, keepdims=False)
        one, two, three = over_ch(mine, 1), over_ch(theirs, 2), over_ch(theirs, 3)
        return (
            jnp.concatenate(by_image(mine, two), axis=1),
            jnp.concatenate(by_image(one, three), axis=1),
        )

    def other_shard(weight):
        rows = weight.shape[0] // blocks
        chunk = lax.dynamic_slice_in_dim(weight, b * rows, rows, 0)
        return lax.all_gather(over_ch(chunk, 2), "blk", axis=0, tiled=True)

    def all_reduce(value):
        if blocks != 8:
            return lax.psum(value.astype(BF), "blk").astype(F32)
        rows = value.shape[0]
        core, chip = b % 2, b // 2
        keep = lax.dynamic_slice_in_dim(value, core * (rows // 2), rows // 2, 0)
        send = lax.dynamic_slice_in_dim(value, (1 - core) * (rows // 2), rows // 2, 0)
        part = keep.astype(F32) + over_blk(send.astype(BF), 1).astype(F32)
        part = part.reshape(4, rows // 8, LANES)
        total = lax.dynamic_index_in_dim(part, chip, 0, keepdims=False)
        for mask in (3, 1, 2):
            chunk = lax.dynamic_index_in_dim(part, chip ^ mask, 0, keepdims=False)
            total = total + over_blk(chunk.astype(BF), 2 * mask).astype(F32)
        total = total.astype(BF)
        rel = jnp.stack([total] + [over_blk(total, 2 * mask) for mask in (1, 2, 3)])
        half = jnp.concatenate(
            [lax.dynamic_index_in_dim(rel, n ^ chip, 0, keepdims=False) for n in range(4)], axis=0
        )
        other = over_blk(half, 1)
        first = jnp.where(core == 0, half, other)
        second = jnp.where(core == 0, other, half)
        return jnp.concatenate([first, second], axis=0).astype(F32)

    emb_act = embed_features(timesteps, image_embed).astype(BF)
    scale_shift = (
        jnp.einsum("ie,esc->isc", emb_act, embed_weight, preferred_element_type=F32) + embed_bias
    )
    local_vec = jnp.concatenate(
        [
            jnp.stack([norm1_gain, norm1_bias, norm2_gain, norm2_bias, norm3_gain, norm3_bias]),
            scale_shift.reshape(4, width),
            jnp.zeros((6, width), F32),
        ],
        axis=0,
    )
    all_vec = lax.all_gather(local_vec, "ch", axis=0)
    emb_rows = lax.dynamic_slice_in_dim(all_vec, 6 + 2 * i, 2, 1)
    vec = jnp.concatenate([all_vec[:, :6], emb_rows], axis=1)

    x_own, x_oth = halves(block_input)
    w1_own = conv1_weight.reshape(-1, width)
    w1_oth = other_shard(w1_own)
    x_all = jnp.concatenate([x_own, x_oth], axis=1)
    x_top, x_bot = halo_rows(x_all)
    x_f = x_all.astype(F32)
    zeros6 = jnp.zeros((6, channels), F32)
    sums1 = blk_sum(
        jnp.concatenate([jnp.sum(x_f, axis=0)[None], jnp.sum(x_f * x_f, axis=0)[None], zeros6])
    )
    w2_own = conv2_weight.reshape(-1, width)
    w2_oth = other_shard(w2_own)
    heads = lambda v: v.reshape(channels, 2, HEAD)
    wp_own = jnp.concatenate(
        [
            heads(qkv_weight[:, 1]),
            heads(qkv_weight[:, 2]),
            heads(qkv_weight[:, 0] * 0.125),
            heads(out_weight.T),
        ],
        axis=2,
    ).reshape(channels, 2 * HALF)
    wp_oth = over_ch(wp_own, 2)
    cot_own, cot_oth = halves(cotangent)
    cot_top, cot_bot = halo_rows(cot_own)

    j = b // split
    ctx_rows = -(-ctx_len // 16) * 16
    ctx_w = jnp.stack(
        [
            lax.dynamic_slice_in_dim(
                ctx_weight, 128 * (hh + 2 * (j // 2)) + HEAD * (j % 2), HEAD, 2
            ).reshape(-1, 2 * HEAD)
            for hh in range(2)
        ]
    )
    ctx_term = jnp.einsum("itx,hxk->ihtk", context, ctx_w, preferred_element_type=F32)
    ctx_kv = lax.psum_scatter(
        ctx_term.astype(BF).reshape(4, ctx_len, 2 * HEAD), "ch", scatter_dimension=0
    )
    ctx_kv = jnp.pad(ctx_kv, ((0, ctx_rows - ctx_len), (0, 0)))
    live = (CLIPTOK + lax.dynamic_slice_in_dim(text_len, i, 1, 0)).astype(jnp.int32)

    conv_flops = 2 * pix * 9 * channels * HALF
    ext_rows = pix + 2 * COLS
    kind = dict(cells=cells, size=size)
    w_scratch = ((9 * channels, HALF), BF)

    hid_own, hid_part, act1 = call(
        functools.partial(conv_kernel, which=0, **kind),
        [scal, x_own, x_oth, x_top, x_bot, sums1, vec, w1_own, w1_oth],
        [((pix, HALF), BF), ((8, HALF), F32), ((pix, channels), BF)],
        [((ext_rows, channels), BF), w_scratch],
        conv_flops,
    )
    hid_oth = over_ch(hid_own, 1)
    hid_top, hid_bot = halo_rows(jnp.concatenate([hid_own, hid_oth], axis=1))
    hid_sum = blk_sum(hid_part)
    sums2 = jnp.concatenate([hid_sum, over_ch(hid_sum, 1)], axis=1)

    res_f, res_own, res_part, act2 = call(
        functools.partial(conv_kernel, which=1, **kind),
        [scal, hid_own, hid_oth, hid_top, hid_bot, sums2, vec, w2_own, w2_oth, x_own],
        [((pix, HALF), F32), ((pix, HALF), BF), ((8, HALF), F32), ((pix, channels), BF)],
        [((ext_rows, channels), BF), w_scratch],
        conv_flops,
    )
    res_oth = over_ch(res_own, 1)
    res_sum = blk_sum(res_part)
    sums3 = jnp.concatenate([res_sum, over_ch(res_sum, 1)], axis=1)

    packed, act3, cot_all = call(
        functools.partial(qkv_kernel, **kind),
        [scal, res_own, res_oth, sums3, vec, cot_own, cot_oth, wp_own, wp_oth],
        [((4, pix, HALF), BF), ((pix, channels), BF), ((pix, channels), BF)],
        (),
        4 * pix * channels * 4 * HALF,
    )
    recv = lax.all_to_all(packed.reshape(blocks, pix // split, HALF), "blk", 0, 0)
    recv = recv.reshape(-1, HALF)
    queries = recv.shape[0]
    if split == 2:
        kva, kvb = recv, over_blk(recv[:, :LANES], 1)
    else:
        groups = [[n * split + m for m in range(split)] for n in range(4)]
        kv_all = lax.all_gather(
            recv[:, :LANES], "blk", axis=0, tiled=True, axis_index_groups=groups
        )
        kva, kvb = kv_all[: kv_all.shape[0] // 2], kv_all[kv_all.shape[0] // 2 :]
    dqo, dkva, dkvb, dctx = attend(live, recv, kva, kvb, ctx_kv)
    if split == 2:
        d_kv = dkva + over_blk(dkvb, 1).astype(F32)
        d_ctx = dctx + over_blk(dctx, 1)
    else:
        d_kv = lax.psum_scatter(
            jnp.concatenate([dkva, dkvb.astype(F32)], axis=0),
            "blk",
            scatter_dimension=0,
            axis_index_groups=groups,
            tiled=True,
        )
        d_ctx = lax.psum(dctx, "blk", axis_index_groups=groups)
    back = jnp.concatenate([d_kv.astype(BF), dqo], axis=1)
    grads = lax.all_to_all(back.reshape(blocks, pix // split, HALF), "blk", 0, 0)
    grads = grads.reshape(4, pix, HALF)

    p3_own, p3_oth, st3 = call(
        functools.partial(qkv_back_kernel, **kind),
        [scal, grads, wp_own, wp_oth, res_own, res_oth, sums3, vec],
        [((pix, HALF), F32), ((pix, HALF), BF), ((8, channels), F32)],
        [((pix, channels), F32)],
        2 * pix * channels * 4 * HALF,
    )

    def exchange(part_own, part_oth, stats):
        recv_part = over_ch(part_oth, 1)
        own_stats = stats[:, :HALF] + over_ch(stats[:, HALF:], 1)
        first = (part_own[:COLS] + recv_part[:COLS].astype(F32)).astype(BF)
        last = (part_own[pix - COLS :] + recv_part[pix - COLS :].astype(F32)).astype(BF)
        return recv_part, first, last, blk_sum(own_stats)

    r3, first3, last3, stats3 = exchange(p3_own, p3_oth, st3)
    d_top3, d_bot3 = halo(first3, last3)
    res_top, res_bot = halo_rows(res_own)
    low_grad = [((pix, HALF), F32), ((pix, HALF), BF), ((8, channels), F32)]
    d_resid, ext2, p2_own, p2_oth, st2 = call(
        functools.partial(conv_back_kernel, which=2, **kind),
        [
            scal, p3_own, r3, d_top3, d_bot3, res_own, res_top, res_bot, res_sum, stats3, vec,
            w2_own, w2_oth, hid_own, hid_oth, sums2, cot_own, cot_top, cot_bot,
        ],
        [((pix, HALF), F32), ((ext_rows, HALF), BF)] + low_grad,
        [w_scratch, ((pix, channels), F32)],
        conv_flops,
    )
    r2, first2, last2, stats2 = exchange(p2_own, p2_oth, st2)
    d_top2, d_bot2 = halo(first2, last2)
    ext1, p1_own, p1_oth, st1 = call(
        functools.partial(conv_back_kernel, which=1, **kind),
        [
            scal, p2_own, r2, d_top2, d_bot2, hid_own, hid_top[:, :HALF], hid_bot[:, :HALF],
            hid_sum, stats2, vec, w1_own, w1_oth, x_own, x_oth, sums1,
        ],
        [((ext_rows, HALF), BF)] + low_grad,
        [w_scratch, ((pix, channels), F32)],
        conv_flops,
    )

    def conv_weight_grad(act, ext):
        shard_parts = by_image(ext[:, :LANES], ext[:, LANES:])
        act_there = over_ch(act, 2)
        ext_there = over_ch(shard_parts[1], 2)
        return call(
            weight_grad_kernel,
            [act, act_there, shard_parts[0], ext_there],
            [((9 * channels, width), F32)],
            [((pix, 9 * LANES), BF)],
            conv_flops,
            scalars=0,
        )[0]

    grad1_part = conv_weight_grad(act1, ext1)
    grad2_part = conv_weight_grad(act2, ext2)

    recv_part1 = over_ch(p1_oth, 1)
    stats1 = blk_sum(st1[:, :HALF] + over_ch(st1[:, HALF:], 1))
    in_keep, in_send = call(
        functools.partial(last_kernel, **kind),
        [scal, p1_own, recv_part1, x_own, sums1[:, :HALF], stats1, vec, d_resid],
        [((pix, width), F32), ((pix, width), BF)],
        [((pix, HALF), F32)],
    )
    input_grad = jnp.stack(by_image(in_keep, over_ch(in_send, 2).astype(F32))).reshape(
        block_input.shape
    )

    proj_own, proj_oth, wp_keep, wp_send = call(
        out_kernel,
        [scal, grads, wp_own, wp_oth, act3, cot_all],
        [
            ((pix, HALF), F32),
            ((pix, HALF), BF),
            ((channels, 2 * HALF), F32),
            ((channels, 2 * HALF), BF),
        ],
        [((pix, channels), F32)],
        6 * pix * channels * 4 * HALF,
    )
    out_own = (res_f + proj_own + over_ch(proj_oth, 1).astype(F32)).astype(BF)
    out_keep, out_send = by_image(out_own[:, :LANES], out_own[:, LANES:])
    block_output = jnp.stack(by_image(out_keep, over_ch(out_send, 2))).reshape(block_input.shape)
    wp_part = wp_keep + over_ch(wp_send, 2).astype(F32)
    grad1 = all_reduce(grad1_part)
    bundle = all_reduce(
        jnp.concatenate([grad2_part, wp_part.reshape(-1, LANES)], axis=0)
    )
    grad2 = bundle[: 9 * channels]
    wp_grad = bundle[9 * channels :].reshape(channels, 2, 4, HEAD)
    qkv_grad = jnp.stack(
        [
            wp_grad[:, :, 2].reshape(channels, width) * 0.125,
            wp_grad[:, :, 0].reshape(channels, width),
            wp_grad[:, :, 1].reshape(channels, width),
        ],
        axis=1,
    )
    out_grad = wp_grad[:, :, 3].reshape(channels, width).T

    def both_images(stats):
        mine, theirs = by_image(stats[:2, :LANES], stats[:2, LANES:])
        return jnp.stack(by_image(mine, over_ch(theirs, 2)))

    ab1, ab2, ab3 = both_images(stats1), both_images(stats2), both_images(stats3)
    grow = 1.0 + scale_shift[:, 0]
    d_shift = ab2[:, 0]
    d_scale = norm2_gain * ab2[:, 1] + norm2_bias * ab2[:, 0]
    d_scale_shift = jnp.stack((d_scale, d_shift), axis=1)
    embed_weight_grad = (
        emb_act[0].astype(F32)[:, None, None] * d_scale_shift[0]
        + emb_act[1].astype(F32)[:, None, None] * d_scale_shift[1]
    )

    d_ctx = lax.all_gather(d_ctx[:ctx_len].astype(BF), "ch", axis=0)
    d_ctx = d_ctx.reshape(images, 2, ctx_len, 2 * HEAD)
    features = context.shape[2] // split
    ctx_part = lax.dynamic_slice_in_dim(context, (b % split) * features, features, 2)
    ctx_partial = jnp.einsum("itx,ihtk->xhk", ctx_part, d_ctx, preferred_element_type=F32)
    ctx_grad = lax.all_gather(ctx_partial.astype(BF), "blk", axis=0)
    ctx_grad = ctx_grad.reshape(2, 2, split, features, 2, 2, HEAD)
    ctx_grad = jnp.transpose(ctx_grad, (2, 3, 5, 0, 4, 1, 6)).astype(F32)

    return (
        block_output,
        input_grad,
        grad1.reshape(conv1_weight.shape),
        grad2.reshape(conv2_weight.shape),
        embed_weight_grad,
        jnp.sum(d_scale_shift, axis=0),
        jnp.sum(ab1[:, 1], axis=0),
        jnp.sum(ab1[:, 0], axis=0),
        jnp.sum(grow * ab2[:, 1], axis=0),
        jnp.sum(grow * ab2[:, 0], axis=0),
        jnp.sum(ab3[:, 1], axis=0),
        jnp.sum(ab3[:, 0], axis=0),
        qkv_grad,
        out_grad,
        ctx_grad.reshape(ctx_weight.shape),
    )


def solution(mesh):
    return jax.shard_map(
        body,
        mesh=mesh,
        in_specs=(
            P(None, "blk", None, "ch"),
            P(None, "blk", None, "ch"),
            P(),
            P(),
            P(),
            P(None, None, "ch"),
            P(None, None, None, "ch"),
            P(None, None, None, "ch"),
            P(None, None, "ch"),
            P(None, "ch"),
            P("ch"),
            P("ch"),
            P("ch"),
            P("ch"),
            P("ch"),
            P("ch"),
            P(None, None, "ch"),
            P("ch", None),
            P("ch", None, None),
        ),
        out_specs=(
            P(None, "blk", None, "ch"),
            P(None, "blk", None, "ch"),
            P(None, None, None, "ch"),
            P(None, None, None, "ch"),
            P(None, None, "ch"),
            P(None, "ch"),
            P("ch"),
            P("ch"),
            P("ch"),
            P("ch"),
            P("ch"),
            P("ch"),
            P(None, None, "ch"),
            P("ch", None),
            P("ch", None, None),
        ),
        check_vma=False,
    )
```

time: 845 us -> 519 us (0.61)
  matrix products: 203 us -> 2.21 us
  waiting for transfers between devices: 334 us -> 153 us
  starting transfers between devices: 15.4 us -> 118 us
  Pallas kernels: 0 us -> 87.3 us
  blocking collectives: 103 us -> 27.5 us
  local copies, waits for them, and re-layouts: 116 us -> 65 us
  loops' own time: 8.86 us -> 0 us
    dot_general x105 -> x3, matrix products: 203 us -> 2.21 us  [the longest x1 0.97 us: body(): jnp.einsum('itx,ihtk->xhk', ctx_part, d_ctx, preferred_element_type=F32)]
    all_gather x6 -> x3, waiting for transfers between devices: 129 us -> 0.02 us  [the longest x2 0.02 us: other_shard(): return lax.all_gather(over_ch(chunk, 2), 'blk', axis=0, tiled=True)]
    psum x1 -> x0, waiting for transfers between devices: 121 us -> none  [body(): lax.psum((conv1_grad, conv2_grad, embed_weight_grad, embed_bias_grad, gai...]
    ppermute x8 -> x61, waiting for transfers between devices: 1.91 us -> 120 us  [the longest x30 101 us: over_ch(): return lax.ppermute(value, 'ch', [(n, n ^ mask) for n in range(4)])]
    psum x6 -> x0, blocking collectives: 103 us -> none  [group_means(): total_first, total_second = lax.psum((first_g, second_g), 'blk')]
    pallas_call x0 -> x11, Pallas kernels: none -> 87.3 us  [the longest x10 49.4 us: call(): pl.pallas_call(kernel, in_specs=[in_smem] * scalars + [in_vmem] * (len(ar...]
    unnamed x18 -> x5, waiting for transfers between devices: 81.8 us -> 6.6 us
    ppermute x8 -> x61, starting transfers between devices: 14 us -> 78.4 us  [the longest x30 35.2 us: over_ch(): return lax.ppermute(value, 'ch', [(n, n ^ mask) for n in range(4)])]
  transfers between devices with their start and end apart: 21 -> 73, of which waited for: 11 -> 30; matrix products, arithmetic and copies ran while one was open for 26% -> 15% of each run, Pallas kernels for 0% -> 9%
where the time goes in v1:
time: 519 us; the launch traced here: 510 us
  waiting for transfers between devices  153 us (29%)
  starting transfers between devices  118 us (23%)
  Pallas kernels  87.3 us (17%)
  local copies, waits for them, and re-layouts  65 us (13%)
  other arithmetic  39.2 us (8%)
  blocking collectives  27.5 us (5%)
  between operations  17.4 us (3%)
    ppermute x30, waiting for transfers between devices, over_ch(): return lax.ppermute(value, 'ch', [(n, n ^ mask) for n in range(4)])  101 us
    pallas_call x10, Pallas kernels, call(): pl.pallas_call(kernel, in_specs=[in_smem] * scalars + [in_vmem] * (len(ar...  49.4 us
    pallas_call x1, Pallas kernels, attend(): pl.pallas_call(functools.partial(attend_kernel, chunk=512, unroll=4), gri...  37.9 us
    ppermute x30, starting transfers between devices, over_ch(): return lax.ppermute(value, 'ch', [(n, n ^ mask) for n in range(4)])  35.2 us
    all_to_all x6, starting transfers between devices, blk_sum(): return jnp.sum(lax.all_to_all(spread, 'blk', 0, 0), axis=0)  31.3 us
    unnamed x125, local copies, waits for them, and re-layouts  25.7 us
    ppermute x12, starting transfers between devices, halo(): return (lax.ppermute(last, 'blk', up), lax.ppermute(first, 'blk', down))  25.2 us
    ppermute x19, waiting for transfers between devices, over_blk(): return lax.ppermute(value, 'blk', [(n, n ^ mask) for n in range(blocks)])  18.5 us
  transfers between devices with their start and end apart: 73, of which 30 were waited for; matrix products, arithmetic and copies ran while one was open for 15% of the time, Pallas kernels for 9%

profile of v1, /device:TPU:0, one launch (start us, length us, event | category | flops | bytes accessed | tf_op | source)
XLA Modules:
  0.0 509.5 jit_solution(13412519513127900526)
XLA Ops:
  9.8 5.0 collective-permute-start.15
  16.4 1.9 collective-permute-start.2
  20.3 2.0 collective-permute-start.5
  24.1 19.5 %collective-permute-done.5 = bf16[576,128]{1,0:T(8,128)(2,1)S(1)} collective-permute-done((bf16[576,128]{1,0:T(8,128)(2,1)S(1)}, bf16[576,128]{1,0:T(8,128)(2,1)S(1)}, u32[]{:S(2)}, u32[]{:S(2)}) %collective-permute-start.5) | collective-permute-done | bytes 147488 | tf_op jit(solution)/shard_map/ppermute | solution.py:515
  46.7 13.1 %all-gather = f32[64,128]{1,0:T(8,128)S(1)} all-gather(f32[16,128]{1,0:T(8,128)S(1)} %concatenate.65), channel_id=2, replica_groups=mesh['blk'=8,'ch'=4] {'ch'}, dimensions={0}, use_global_device_ids=true | all-gather | bytes 40960 | tf_op jit(solution)/shard_map/all_gather | solution.py:585
  63.1 2.5 collective-permute-start.1
  67.1 7.9 %collective-permute-done.1 = bf16[512,128]{1,0:T(8,128)(2,1)S(1)} collective-permute-done((bf16[512,128]{1,0:T(8,128)(2,1)S(1)}, bf16[512,128]{1,0:T(8,128)(2,1)S(1)}, u32[]{:S(2)}, u32[]{:S(2)}) %collective-permute-start.1) | collective-permute-done | bytes 131104 | tf_op jit(solution)/shard_map/ppermute | solution.py:515
  76.0 4.1 all-to-all-start
  81.4 3.0 collective-permute-start.3
  86.9 5.3 %shard_map.298 = (bf16[512,256]{1,0:T(8,128)(2,1)}, f32[8,256]{1,0:T(8,128)}, bf16[512,512]{1,0:T(8,128)(2,1)}) custom-call(s32[4]{0:T(128)} %pad_add_fusion.scal, bf16[512,256]{1,0:T(8,128)(2,1)} %pad_maximum_fusion.11.own.rest_0_.low_own.field, bf16[512,256]{1,0:T(8,128)(2,1)} %pad_maximum_fusion.12.oth.low_oth, bf16[64,512]{1,0:T(8,128)(2,1)} %copy-done.48, ...), custom_call_target="tpu_custom_call" | custom-call | flops 1207959552 | bytes 3842064 | tf_op jit(solution)/shard_map/pallas_call | solution.py:460
  92.2 2.5 collective-permute-start.6
  96.7 6.8 %all-to-all-start.1 = ((f32[8,8,256]{2,1,0:T(8,128)}), f32[8,8,256]{2,1,0:T(8,128)S(1)}, u32[]{:S(2)}, u32[]{:S(2)}) async-start(f32[8,8,256]{2,1,0:T(8,128)} %broadcast_in_dim.25), calls=%async_computation.1 | async-start | bytes 131072 | tf_op jit(solution)/shard_map/all_to_all | solution.py:530
  104.5 4.0 all-to-all-done.1
  110.0 2.3 collective-permute-done.9
  115.4 5.4 %shard_map.299 = (f32[512,256]{1,0:T(8,128)}, bf16[512,256]{1,0:T(8,128)(2,1)}, f32[8,256]{1,0:T(8,128)}, bf16[512,512]{1,0:T(8,128)(2,1)}) custom-call(s32[4]{0:T(128)} %pad_add_fusion.scal, bf16[512,256]{1,0:T(8,128)(2,1)} %get-tuple-element.47.own.low_own.field, bf16[512,256]{1,0:T(8,128)(2,1)} %copy-done.18, bf16[64,512]{1,0:T(8,128)(2,1)} %copy-done.33, ...), custom_call_target="tpu_custom_call" | custom-call | flops 1207959552 | bytes 4628496 | tf_op jit(solution)/shard_map/pallas_call | solution.py:460
  122.1 5.8 %all-to-all-start.2 = ((f32[8,8,256]{2,1,0:T(8,128)}), f32[8,8,256]{2,1,0:T(8,128)S(1)}, u32[]{:S(2)}, u32[]{:S(2)}) async-start(f32[8,8,256]{2,1,0:T(8,128)} %broadcast_in_dim.26), calls=%async_computation.2 | async-start | bytes 131072 | tf_op jit(solution)/shard_map/all_to_all | solution.py:530
  129.0 3.9 all-to-all-done.2
  134.8 2.2 collective-permute-done.12
  139.1 4.2 shard_map.300
  143.3 4.0 all-to-all-start.3
  149.9 12.8 %all-to-all-done.3 = bf16[8,256,256]{2,1,0:T(8,128)(2,1)S(1)} async-done(((bf16[8,256,256]{2,1,0:T(8,128)(2,1)}), bf16[8,256,256]{2,1,0:T(8,128)(2,1)S(1)}, u32[]{:S(2)}, u32[]{:S(2)}) %all-to-all-start.3) | async-done | bytes 1048608 | tf_op jit(solution)/shard_map/all_to_all | solution.py:667
  164.2 6.5 %reduce-scatter.4.cloned.1.call-done = bf16[1,260,128]{2,1,0:T(8,128)(2,1)} async-done(((bf16[4,260,128]{2,1,0:T(8,128)(2,1)}), bf16[1,260,128]{2,1,0:T(8,128)(2,1)}) %reduce-scatter.4.cloned.1.call-update) | async-done | bytes 66576
  173.1 37.9 %shard_map.301 = (bf16[2048,128]{1,0:T(8,128)(2,1)}, f32[2048,128]{1,0:T(8,128)}, bf16[2048,128]{1,0:T(8,128)(2,1)}, f32[272,128]{1,0:T(8,128)}) custom-call(s32[1]{0:T(128)S(6)} %add.199.live, bf16[2048,256]{1,0:T(8,128)(2,1)} %bitcast.169, bf16[2048,256]{1,0:T(8,128)(2,1)} %bitcast.170, bf16[2048,128]{1,0:T(8,128)(2,1)} %copy-done.44, bf16[272,128]{1,0:T(8,128)(2,1)} %pad.4.ctx), custom_call_target="tpu_custom_call" | custom-call | flops 27481079808 | bytes 4472832 | tf_op jit(solution)/shard_map/pallas_call | solution.py:418
  214.4 3.9 all-to-all-start.4
  219.7 3.0 collective-permute-start.27
  227.1 3.0 collective-permute-start.24
  231.4 14.4 %all-gather.3 = bf16[4,260,128]{2,1,0:T(8,128)(2,1)S(1)} all-gather(bf16[1,260,128]{2,1,0:T(8,128)(2,1)S(1)} %fusion.26), channel_id=3, replica_groups=mesh['blk'=8,'ch'=4] {'ch'}, dimensions={0}, use_global_device_ids=true | all-gather | bytes 332800 | tf_op jit(solution)/shard_map/all_gather | solution.py:811
  246.8 3.4 shard_map.303
  251.9 2.7 collective-permute-done.26
  255.9 4.5 all-to-all-start.5
  260.4 5.0 shard_map.302
  267.7 2.0 collective-permute-start.19
  271.0 3.4 collective-permute-start.22
  280.1 6.0 %shard_map.304 = (f32[512,256]{1,0:T(8,128)}, bf16[640,256]{1,0:T(8,128)(2,1)}, f32[512,256]{1,0:T(8,128)}, bf16[512,256]{1,0:T(8,128)(2,1)}, f32[8,512]{1,0:T(8,128)}) custom-call(s32[4]{0:T(128)} %pad_add_fusion.scal, f32[512,256]{1,0:T(8,128)} %get-tuple-element.60.part_own, bf16[512,256]{1,0:T(8,128)(2,1)} %copy-done.35, bf16[64,256]{1,0:T(8,128)(2,1)} %copy-done.54, ...), custom_call_target="tpu_custom_call" | custom-call | flops 1207959552 | bytes 6094864 | tf_op jit(solution)/shard_map/pallas_call | solution.py:460
  286.9 24.0 %collective-permute-done.32 = f32[8,256]{1,0:T(8,128)S(1)} collective-permute-done((f32[8,256]{1,0:T(8,128)S(1)}, f32[8,256]{1,0:T(8,128)S(1)}, u32[]{:S(2)}, u32[]{:S(2)}) %collective-permute-start.32) | collective-permute-done | bytes 8224 | tf_op jit(solution)/shard_map/ppermute | solution.py:515
  312.3 4.1 all-to-all-start.6
  317.7 3.7 all-to-all-done.6
  323.4 28.4 %collective-permute-done.57 = f32[2,128]{1,0:T(2,128)S(1)} collective-permute-done((f32[2,128]{1,0:T(2,128)S(1)}, f32[2,128]{1,0:T(2,128)S(1)}, u32[]{:S(2)}, u32[]{:S(2)}) %collective-permute-start.57) | collective-permute-done | bytes 1056 | tf_op jit(solution)/shard_map/ppermute | solution.py:515
  352.4 8.3 %multiply_add_fusion = f32[2048,2,128]{2,1,0:T(2,128)} fusion(f32[2,128]{1,0:T(2,128)S(1)} %bitcast.220, f32[2,128]{1,0:T(2,128)S(1)} %bitcast.219, f32[2048]{0:T(1024)S(1)} %bitcast.205, f32[2048]{0:T(1024)S(1)} %bitcast.204), kind=kLoop, calls=%fused_computation.4 | loop fusion | flops 1572864 | bytes 2115584 | tf_op jit(solution)/shard_map/add | solution.py:807
  364.5 5.6 %shard_map.308 = f32[4608,128]{1,0:T(8,128)} custom-call(bf16[512,512]{1,0:T(8,128)(2,1)} %get-tuple-element.74.act_one, bf16[512,512]{1,0:T(8,128)(2,1)} %collective-permute-done.46.act_two, bf16[640,128]{1,0:T(8,128)(2,1)} %get-tuple-element.238.ext_one, bf16[640,128]{1,0:T(8,128)(2,1)} %copy-done.46), custom_call_target="tpu_custom_call" | custom-call | flops 1207959552 | bytes 3735552 | tf_op jit(solution)/shard_map/pallas_call | solution.py:460
  372.3 3.6 collective-permute-start.30
  376.9 6.1 %shard_map.305 = (bf16[640,256]{1,0:T(8,128)(2,1)}, f32[512,256]{1,0:T(8,128)}, bf16[512,256]{1,0:T(8,128)(2,1)}, f32[8,512]{1,0:T(8,128)}) custom-call(s32[4]{0:T(128)} %pad_add_fusion.scal, f32[512,256]{1,0:T(8,128)} %get-tuple-element.63.part_own, bf16[512,256]{1,0:T(8,128)(2,1)} %copy-done.36, bf16[64,256]{1,0:T(8,128)(2,1)} %collective-permute-done.30.dtop, ...), custom_call_target="tpu_custom_call" | custom-call | flops 1207959552 | bytes 5242896 | tf_op jit(solution)/shard_map/pallas_call | solution.py:460
  387.4 2.6 copy.195
  390.0 4.0 reshape.201
  394.0 6.7 %copy.202 = f32[2,256,2,2,2,2,64]{6,5,4,3,2,1,0:T(2,128)} copy(f32[2,256,2,2,2,2,64]{1,0,5,3,6,2,4:T(2,128)} %bitcast.159) | data formatting | bytes 4194304
  400.7 6.4 %reshape.217 = f32[512,2,512]{2,1,0:T(2,128)} reshape(f32[2,256,2,2,2,2,64]{6,5,4,3,2,1,0:T(2,128)} %copy.202) | data formatting | bytes 4194304
  407.7 5.9 %all-to-all-start.7 = ((f32[8,8,256]{2,1,0:T(8,128)}), f32[8,8,256]{2,1,0:T(8,128)S(1)}, u32[]{:S(2)}, u32[]{:S(2)}) async-start(f32[8,8,256]{2,1,0:T(8,128)} %broadcast_in_dim.29), calls=%async_computation.7 | async-start | bytes 131072 | tf_op jit(solution)/shard_map/all_to_all | solution.py:530
  420.1 6.7 %collective-permute-done.37.ext_two = bf16[640,128]{1,0:T(8,128)(2,1)} collective-permute-done((bf16[640,128]{1,0:T(8,128)(2,1)}, bf16[640,128]{1,0:T(8,128)(2,1)}, u32[]{:S(2)}, u32[]{:S(2)}) %collective-permute-start.37) | collective-permute-done | bytes 163872 | tf_op jit(solution)/shard_map/ppermute | solution.py:515
  426.9 5.5 %shard_map.307 = f32[4608,128]{1,0:T(8,128)} custom-call(bf16[512,512]{1,0:T(8,128)(2,1)} %get-tuple-element.72.act_one, bf16[512,512]{1,0:T(8,128)(2,1)} %collective-permute-done.36.act_two, bf16[640,128]{1,0:T(8,128)(2,1)} %get-tuple-element.240.ext_one, bf16[640,128]{1,0:T(8,128)(2,1)} %collective-permute-done.37.ext_two), custom_call_target="tpu_custom_call" | custom-call | flops 1207959552 | bytes 3735552 | tf_op jit(solution)/shard_map/pallas_call | solution.py:460
  433.8 3.1 shard_map.306
  438.1 7.3 %collective-permute-done.35 = bf16[512,128]{1,0:T(8,128)(2,1)S(1)} collective-permute-done((bf16[512,128]{1,0:T(8,128)(2,1)}, bf16[512,128]{1,0:T(8,128)(2,1)S(1)}, u32[]{:S(2)}, u32[]{:S(2)}) %collective-permute-start.35) | collective-permute-done | bytes 131104 | tf_op jit(solution)/shard_map/ppermute | solution.py:515
  447.5 2.6 collective-permute-start.39
  451.0 2.0 fusion.3
  453.1 2.6 collective-permute-start.50
  458.8 2.3 collective-permute-start.44
  464.6 4.4 collective-permute-done.52
  470.3 2.0 collective-permute-start.54
  474.6 3.9 collective-permute-done.55
  478.5 3.5 collective-permute-done.54
  486.7 2.0 maximum_convert_fusion
  488.7 2.2 reshape.188
  490.9 2.5 fusion.44
  493.4 1.9 copy.192
  499.0 3.2 slice.263
  (353 shorter events, 110.7 us)
Async XLA Ops:
  8.0 78.2 %all-gather.8.cloned.1.call-start = ((), (), s32[]{:S(2)}) async-start(), calls=%async_computation.9 | async-start | bytes 1327104 | tf_op jit(solution)/shard_map/all_gather | solution.py:548
  9.8 119.2 %collective-permute-start.15 = (bf16[512,128]{1,0:T(8,128)(2,1)}, bf16[512,128]{1,0:T(8,128)(2,1)S(1)}, u32[]{:S(2)}, u32[]{:S(2)}) collective-permute-start(bf16[512,128]{1,0:T(8,128)(2,1)} %dynamic-slice_bitcast_fusion.8), channel_id=1, source_target_pairs={{0,3},{1,2},{2,1},{3,0},{4,7},{5,6},{6,5},{7,4},{8,11},{9,10},{10,... | collective-permute-start | bytes 393224 | tf_op jit(solution)/shard_map/ppermute | solution.py:515
  14.8 48.3 %collective-permute-start.13 = (bf16[512,128]{1,0:T(8,128)(2,1)}, bf16[512,128]{1,0:T(8,128)(2,1)S(1)}, u32[]{:S(2)}, u32[]{:S(2)}) collective-permute-start(bf16[512,128]{1,0:T(8,128)(2,1)} %dynamic-slice_bitcast_fusion.8), channel_id=1, source_target_pairs={{0,2},{1,3},{2,0},{3,1},{4,6},{5,7},{6,4},{7,5},{8,10},{9,11},{10,... | collective-permute-start | bytes 393224 | tf_op jit(solution)/shard_map/ppermute | solution.py:515
  16.4 50.7 %collective-permute-start.2 = (bf16[512,128]{1,0:T(8,128)(2,1)}, bf16[512,128]{1,0:T(8,128)(2,1)S(1)}, u32[]{:S(2)}, u32[]{:S(2)}) collective-permute-start(bf16[512,128]{1,0:T(8,128)(2,1)} %dynamic-slice_bitcast_fusion.10), channel_id=1, source_target_pairs={{0,3},{1,2},{2,1},{3,0},{4,7},{5,6},{6,5},{7,4},{8,11},{9,10},{10,... | collective-permute-start | bytes 393224 | tf_op jit(solution)/shard_map/ppermute | solution.py:515
  18.3 44.2 %collective-permute-start = (bf16[512,128]{1,0:T(8,128)(2,1)}, bf16[512,128]{1,0:T(8,128)(2,1)S(1)}, u32[]{:S(2)}, u32[]{:S(2)}) collective-permute-start(bf16[512,128]{1,0:T(8,128)(2,1)} %dynamic-slice_bitcast_fusion.10), channel_id=1, source_target_pairs={{0,2},{1,3},{2,0},{3,1},{4,6},{5,7},{6,4},{7,5},{8,10},{9,11},{10,... | collective-permute-start | bytes 393224 | tf_op jit(solution)/shard_map/ppermute | solution.py:515
  20.3 23.3 %collective-permute-start.5 = (bf16[576,128]{1,0:T(8,128)(2,1)S(1)}, bf16[576,128]{1,0:T(8,128)(2,1)S(1)}, u32[]{:S(2)}, u32[]{:S(2)}) collective-permute-start(bf16[576,128]{1,0:T(8,128)(2,1)S(1)} %constant_dynamic-slice_fusion.3), channel_id=1, source_target_pairs={{0,2},{1,3},{2,0},{3,1},{4,6},{5,7},{6,4},{7,5},{8,10},{9,11},{10,... | collective-permute-start | bytes 442376 | tf_op jit(solution)/shard_map/ppermute | solution.py:515
  43.7 22.0 %collective-permute-start.10 = (bf16[576,128]{1,0:T(8,128)(2,1)S(1)}, bf16[576,128]{1,0:T(8,128)(2,1)S(1)}, u32[]{:S(2)}, u32[]{:S(2)}) collective-permute-start(bf16[576,128]{1,0:T(8,128)(2,1)S(1)} %constant_dynamic-slice_fusion.2), channel_id=1, source_target_pairs={{0,2},{1,3},{2,0},{3,1},{4,6},{5,7},{6,4},{7,5},{8,10},{9,11},{10,... | collective-permute-start | bytes 442376 | tf_op jit(solution)/shard_map/ppermute | solution.py:515
  44.3 69.8 %all-gather.10.cloned.1.call-start = ((), (), s32[]{:S(2)}) async-start(), calls=%async_computation.10 | async-start | bytes 1327104 | tf_op jit(solution)/shard_map/all_gather | solution.py:548
  62.5 75.2 %collective-permute-start.16 = (bf16[512,512]{1,0:T(8,128)(2,1)S(1)}, bf16[512,512]{1,0:T(8,128)(2,1)S(1)}, u32[]{:S(2)}, u32[]{:S(2)}) collective-permute-start(bf16[512,512]{1,0:T(8,128)(2,1)S(1)} %copy.201.own_w), channel_id=1, source_target_pairs={{0,2},{1,3},{2,0},{3,1},{4,6},{5,7},{6,4},{7,5},{8,10},{9,11},{10,... | collective-permute-start | bytes 1572872 | tf_op jit(solution)/shard_map/ppermute | solution.py:515
  63.1 11.9 %collective-permute-start.1 = (bf16[512,128]{1,0:T(8,128)(2,1)S(1)}, bf16[512,128]{1,0:T(8,128)(2,1)S(1)}, u32[]{:S(2)}, u32[]{:S(2)}) collective-permute-start(bf16[512,128]{1,0:T(8,128)(2,1)S(1)} %get-tuple-element.197), channel_id=1, source_target_pairs={{0,1},{1,0},{2,3},{3,2},{4,5},{5,4},{6,7},{7,6},{8,9},{9,8},{10,11... | collective-permute-start | bytes 393224 | tf_op jit(solution)/shard_map/ppermute | solution.py:515
  65.7 63.3 %collective-permute-start.14 = (bf16[512,128]{1,0:T(8,128)(2,1)S(1)}, bf16[512,128]{1,0:T(8,128)(2,1)S(1)}, u32[]{:S(2)}, u32[]{:S(2)}) collective-permute-start(bf16[512,128]{1,0:T(8,128)(2,1)S(1)} %get-tuple-element.194), channel_id=1, source_target_pairs={{0,1},{1,0},{2,3},{3,2},{4,5},{5,4},{6,7},{7,6},{8,9},{9,8},{10,11... | collective-permute-start | bytes 393224 | tf_op jit(solution)/shard_map/ppermute | solution.py:515
  76.0 9.6 %all-to-all-start = ((f32[8,8,512]{2,1,0:T(8,128)}), f32[8,8,512]{2,1,0:T(8,128)S(1)}, u32[]{:S(2)}, u32[]{:S(2)}) async-start(f32[8,8,512]{2,1,0:T(8,128)} %broadcast_in_dim.23), calls=%async_computation | async-start | bytes 262144 | tf_op jit(solution)/shard_map/all_to_all | solution.py:530
  80.1 6.1 %collective-permute-start.4 = (bf16[64,512]{1,0:T(8,128)(2,1)S(1)}, bf16[64,512]{1,0:T(8,128)(2,1)S(1)}, u32[]{:S(2)}, u32[]{:S(2)}) collective-permute-start(bf16[64,512]{1,0:T(8,128)(2,1)S(1)} %get-tuple-element.228), channel_id=1, source_target_pairs={{4,0},{8,4},{12,8},{16,12},{20,16},{24,20},{28,24},{5,1},{9,5},{13... | collective-permute-start | bytes 196616 | tf_op jit(solution)/shard_map/ppermute | solution.py:523
  92.2 16.5 %collective-permute-start.6 = (bf16[512,256]{1,0:T(8,128)(2,1)}, bf16[512,256]{1,0:T(8,128)(2,1)S(1)}, u32[]{:S(2)}, u32[]{:S(2)}) collective-permute-start(bf16[512,256]{1,0:T(8,128)(2,1)} %get-tuple-element.47.own.low_own.field), channel_id=1, source_target_pairs={{0,1},{1,0},{2,3},{3,2},{4,5},{5,4},{6,7},{7,6},{8,9},{9,8},{10,11... | collective-permute-start | bytes 786440 | tf_op jit(solution)/shard_map/ppermute | solution.py:515
  96.7 11.8 %all-to-all-start.1 = ((f32[8,8,256]{2,1,0:T(8,128)}), f32[8,8,256]{2,1,0:T(8,128)S(1)}, u32[]{:S(2)}, u32[]{:S(2)}) async-start(f32[8,8,256]{2,1,0:T(8,128)} %broadcast_in_dim.25), calls=%async_computation.1 | async-start | bytes 131072 | tf_op jit(solution)/shard_map/all_to_all | solution.py:530
  108.7 5.5 %collective-permute-start.8 = (bf16[64,512]{1,0:T(8,128)(2,1)S(1)}, bf16[64,512]{1,0:T(8,128)(2,1)S(1)}, u32[]{:S(2)}, u32[]{:S(2)}) collective-permute-start(bf16[64,512]{1,0:T(8,128)(2,1)S(1)} %get-tuple-element.226), channel_id=1, source_target_pairs={{4,0},{8,4},{12,8},{16,12},{20,16},{24,20},{28,24},{5,1},{9,5},{13... | collective-permute-start | bytes 196616 | tf_op jit(solution)/shard_map/ppermute | solution.py:523
  122.1 10.8 %all-to-all-start.2 = ((f32[8,8,256]{2,1,0:T(8,128)}), f32[8,8,256]{2,1,0:T(8,128)S(1)}, u32[]{:S(2)}, u32[]{:S(2)}) async-start(f32[8,8,256]{2,1,0:T(8,128)} %broadcast_in_dim.26), calls=%async_computation.2 | async-start | bytes 131072 | tf_op jit(solution)/shard_map/all_to_all | solution.py:530
  127.9 9.7 %collective-permute-start.11 = (bf16[512,256]{1,0:T(8,128)(2,1)}, bf16[512,256]{1,0:T(8,128)(2,1)S(1)}, u32[]{:S(2)}, u32[]{:S(2)}) collective-permute-start(bf16[512,256]{1,0:T(8,128)(2,1)} %get-tuple-element.50.own.field), channel_id=1, source_target_pairs={{0,1},{1,0},{2,3},{3,2},{4,5},{5,4},{6,7},{7,6},{8,9},{9,8},{10,11... | collective-permute-start | bytes 786440 | tf_op jit(solution)/shard_map/ppermute | solution.py:515
  143.3 19.4 %all-to-all-start.3 = ((bf16[8,256,256]{2,1,0:T(8,128)(2,1)}), bf16[8,256,256]{2,1,0:T(8,128)(2,1)S(1)}, u32[]{:S(2)}, u32[]{:S(2)}) async-start(bf16[8,256,256]{2,1,0:T(8,128)(2,1)} %bitcast.173), calls=%async_computation.3 | async-start | bytes 2097152 | tf_op jit(solution)/shard_map/all_to_all | solution.py:667
  147.3 23.4 %reduce-scatter.4.cloned.1.call-start = ((), (), s32[]{:S(2)}) async-start(), calls=%async_computation.12 | async-start | bytes 337920
  162.8 9.5 %collective-permute-start.17 = (bf16[2048,128]{1,0:T(8,128)(2,1)S(1)}, bf16[2048,128]{1,0:T(8,128)(2,1)S(1)}, u32[]{:S(2)}, u32[]{:S(2)}) collective-permute-start(bf16[2048,128]{1,0:T(8,128)(2,1)S(1)} %slice.249), channel_id=1, source_target_pairs={{0,4},{4,0},{8,12},{12,8},{16,20},{20,16},{24,28},{28,24},{1,5},{5... | collective-permute-start | bytes 1572872 | tf_op jit(solution)/shard_map/ppermute | solution.py:518
  214.4 31.4 %all-to-all-start.4 = ((bf16[8,256,256]{2,1,0:T(8,128)(2,1)}), bf16[8,256,256]{2,1,0:T(8,128)(2,1)S(1)}, u32[]{:S(2)}, u32[]{:S(2)}) async-start(bf16[8,256,256]{2,1,0:T(8,128)(2,1)} %bitcast.39), calls=%async_computation.4 | async-start | bytes 2097152 | tf_op jit(solution)/shard_map/all_to_all | solution.py:692
  218.3 169.1 %all-gather.12.cloned.1.call-start = ((), (), s32[]{:S(2)}) async-start(), calls=%async_computation.11 | async-start | bytes 1179648 | tf_op jit(solution)/shard_map/all_gather | solution.py:816
  218.4 49.3 %collective-permute-start.28 = (bf16[64,256]{1,0:T(8,128)(2,1)S(1)}, bf16[64,256]{1,0:T(8,128)(2,1)S(1)}, u32[]{:S(2)}, u32[]{:S(2)}) collective-permute-start(bf16[64,256]{1,0:T(8,128)(2,1)S(1)} %get-tuple-element.241), channel_id=1, source_target_pairs={{4,0},{8,4},{12,8},{16,12},{20,16},{24,20},{28,24},{5,1},{9,5},{13... | collective-permute-start | bytes 98312 | tf_op jit(solution)/shard_map/ppermute | solution.py:523
  219.7 50.1 %collective-permute-start.27 = (bf16[64,256]{1,0:T(8,128)(2,1)S(1)}, bf16[64,256]{1,0:T(8,128)(2,1)S(1)}, u32[]{:S(2)}, u32[]{:S(2)}) collective-permute-start(bf16[64,256]{1,0:T(8,128)(2,1)S(1)} %get-tuple-element.242), channel_id=1, source_target_pairs={{0,4},{4,8},{8,12},{12,16},{16,20},{20,24},{24,28},{1,5},{5,9},{9,... | collective-permute-start | bytes 98312 | tf_op jit(solution)/shard_map/ppermute | solution.py:523
  223.3 8.0 %collective-permute-start.60 = (f32[272,128]{1,0:T(8,128)S(1)}, f32[272,128]{1,0:T(8,128)S(1)}, u32[]{:S(2)}, u32[]{:S(2)}) collective-permute-start(f32[272,128]{1,0:T(8,128)S(1)} %copy-done.23), channel_id=1, source_target_pairs={{0,4},{4,0},{8,12},{12,8},{16,20},{20,16},{24,28},{28,24},{1,5},{5... | collective-permute-start | bytes 417800 | tf_op jit(solution)/shard_map/ppermute | solution.py:518
  225.8 48.7 %collective-permute-start.25 = (bf16[64,256]{1,0:T(8,128)(2,1)S(1)}, bf16[64,256]{1,0:T(8,128)(2,1)S(1)}, u32[]{:S(2)}, u32[]{:S(2)}) collective-permute-start(bf16[64,256]{1,0:T(8,128)(2,1)S(1)} %get-tuple-element.243), channel_id=1, source_target_pairs={{4,0},{8,4},{12,8},{16,12},{20,16},{24,20},{28,24},{5,1},{9,5},{13... | collective-permute-start | bytes 98312 | tf_op jit(solution)/shard_map/ppermute | solution.py:523
  227.1 49.2 %collective-permute-start.24 = (bf16[64,256]{1,0:T(8,128)(2,1)S(1)}, bf16[64,256]{1,0:T(8,128)(2,1)S(1)}, u32[]{:S(2)}, u32[]{:S(2)}) collective-permute-start(bf16[64,256]{1,0:T(8,128)(2,1)S(1)} %get-tuple-element.244), channel_id=1, source_target_pairs={{0,4},{4,8},{8,12},{12,16},{16,20},{20,24},{24,28},{1,5},{5,9},{9,... | collective-permute-start | bytes 98312 | tf_op jit(solution)/shard_map/ppermute | solution.py:523
  254.6 10.9 %collective-permute-start.21 = (bf16[512,256]{1,0:T(8,128)(2,1)}, bf16[512,256]{1,0:T(8,128)(2,1)S(1)}, u32[]{:S(2)}, u32[]{:S(2)}) collective-permute-start(bf16[512,256]{1,0:T(8,128)(2,1)} %get-tuple-element.61), channel_id=1, source_target_pairs={{0,1},{1,0},{2,3},{3,2},{4,5},{5,4},{6,7},{7,6},{8,9},{9,8},{10,11... | collective-permute-start | bytes 786440 | tf_op jit(solution)/shard_map/ppermute | solution.py:515
  255.9 9.6 %all-to-all-start.5 = ((f32[8,8,256]{2,1,0:T(8,128)}), f32[8,8,256]{2,1,0:T(8,128)S(1)}, u32[]{:S(2)}, u32[]{:S(2)}) async-start(f32[8,8,256]{2,1,0:T(8,128)} %broadcast_in_dim.27), calls=%async_computation.5 | async-start | bytes 131072 | tf_op jit(solution)/shard_map/all_to_all | solution.py:530
  265.5 5.5 %collective-permute-start.59 = (f32[2,128]{1,0:T(2,128)S(1)}, f32[2,128]{1,0:T(2,128)S(1)}, u32[]{:S(2)}, u32[]{:S(2)}) collective-permute-start(f32[2,128]{1,0:T(2,128)S(1)} %broadcast_select_fusion.20), channel_id=1, source_target_pairs={{0,2},{1,3},{2,0},{3,1},{4,6},{5,7},{6,4},{7,5},{8,10},{9,11},{10,... | collective-permute-start | bytes 3080 | tf_op jit(solution)/shard_map/ppermute | solution.py:515
  267.7 19.1 %collective-permute-start.19 = (bf16[512,256]{1,0:T(8,128)(2,1)}, bf16[512,256]{1,0:T(8,128)(2,1)S(1)}, u32[]{:S(2)}, u32[]{:S(2)}) collective-permute-start(bf16[512,256]{1,0:T(8,128)(2,1)} %get-tuple-element.59), channel_id=1, source_target_pairs={{0,1},{1,0},{2,3},{3,2},{4,5},{5,4},{6,7},{7,6},{8,9},{9,8},{10,11... | collective-permute-start | bytes 786440 | tf_op jit(solution)/shard_map/ppermute | solution.py:515
  269.7 7.8 %collective-permute-start.23 = (bf16[64,256]{1,0:T(8,128)(2,1)S(1)}, bf16[64,256]{1,0:T(8,128)(2,1)S(1)}, u32[]{:S(2)}, u32[]{:S(2)}) collective-permute-start(bf16[64,256]{1,0:T(8,128)(2,1)S(1)} %get-tuple-element.220), channel_id=1, source_target_pairs={{4,0},{8,4},{12,8},{16,12},{20,16},{24,20},{28,24},{5,1},{9,5},{13... | collective-permute-start | bytes 98312 | tf_op jit(solution)/shard_map/ppermute | solution.py:523
  271.0 8.4 %collective-permute-start.22 = (bf16[64,256]{1,0:T(8,128)(2,1)S(1)}, bf16[64,256]{1,0:T(8,128)(2,1)S(1)}, u32[]{:S(2)}, u32[]{:S(2)}) collective-permute-start(bf16[64,256]{1,0:T(8,128)(2,1)S(1)} %get-tuple-element.221), channel_id=1, source_target_pairs={{0,4},{4,8},{8,12},{12,16},{16,20},{20,24},{24,28},{1,5},{5,9},{9,... | collective-permute-start | bytes 98312 | tf_op jit(solution)/shard_map/ppermute | solution.py:523
  274.5 145.6 %collective-permute-start.36 = (bf16[512,512]{1,0:T(8,128)(2,1)}, bf16[512,512]{1,0:T(8,128)(2,1)}, u32[]{:S(2)}, u32[]{:S(2)}) collective-permute-start(bf16[512,512]{1,0:T(8,128)(2,1)} %get-tuple-element.72.act_one), channel_id=1, source_target_pairs={{0,2},{1,3},{2,0},{3,1},{4,6},{5,7},{6,4},{7,5},{8,10},{9,11},{10,... | collective-permute-start | bytes 1572872 | tf_op jit(solution)/shard_map/ppermute | solution.py:515
  276.3 87.5 %collective-permute-start.46 = (bf16[512,512]{1,0:T(8,128)(2,1)S(1)}, bf16[512,512]{1,0:T(8,128)(2,1)}, u32[]{:S(2)}, u32[]{:S(2)}) collective-permute-start(bf16[512,512]{1,0:T(8,128)(2,1)S(1)} %copy-done.43), channel_id=1, source_target_pairs={{0,2},{1,3},{2,0},{3,1},{4,6},{5,7},{6,4},{7,5},{8,10},{9,11},{10,... | collective-permute-start | bytes 1572872 | tf_op jit(solution)/shard_map/ppermute | solution.py:515
  277.6 98.4 %collective-permute-start.48 = (bf16[512,512]{1,0:T(8,128)(2,1)}, bf16[512,512]{1,0:T(8,128)(2,1)S(1)}, u32[]{:S(2)}, u32[]{:S(2)}) collective-permute-start(bf16[512,512]{1,0:T(8,128)(2,1)} %get-tuple-element.77), channel_id=1, source_target_pairs={{0,2},{1,3},{2,0},{3,1},{4,6},{5,7},{6,4},{7,5},{8,10},{9,11},{10,... | collective-permute-start | bytes 1572872 | tf_op jit(solution)/shard_map/ppermute | solution.py:515
  286.8 24.2 %collective-permute-start.32 = (f32[8,256]{1,0:T(8,128)S(1)}, f32[8,256]{1,0:T(8,128)S(1)}, u32[]{:S(2)}, u32[]{:S(2)}) collective-permute-start(f32[8,256]{1,0:T(8,128)S(1)} %slice.212), channel_id=1, source_target_pairs={{0,1},{1,0},{2,3},{3,2},{4,5},{5,4},{6,7},{7,6},{8,9},{9,8},{10,11... | collective-permute-start | bytes 24584 | tf_op jit(solution)/shard_map/ppermute | solution.py:515
  312.3 9.1 %all-to-all-start.6 = ((f32[8,8,256]{2,1,0:T(8,128)}), f32[8,8,256]{2,1,0:T(8,128)S(1)}, u32[]{:S(2)}, u32[]{:S(2)}) async-start(f32[8,8,256]{2,1,0:T(8,128)} %broadcast_in_dim.28), calls=%async_computation.6 | async-start | bytes 131072 | tf_op jit(solution)/shard_map/all_to_all | solution.py:530
  316.4 44.9 %collective-permute-start.20 = (bf16[512,128]{1,0:T(8,128)(2,1)S(1)}, bf16[512,128]{1,0:T(8,128)(2,1)S(1)}, u32[]{:S(2)}, u32[]{:S(2)}) collective-permute-start(bf16[512,128]{1,0:T(8,128)(2,1)S(1)} %broadcast_select_fusion.10), channel_id=1, source_target_pairs={{0,2},{1,3},{2,0},{3,1},{4,6},{5,7},{6,4},{7,5},{8,10},{9,11},{10,... | collective-permute-start | bytes 393224 | tf_op jit(solution)/shard_map/ppermute | solution.py:515
  321.5 30.4 %collective-permute-start.57 = (f32[2,128]{1,0:T(2,128)S(1)}, f32[2,128]{1,0:T(2,128)S(1)}, u32[]{:S(2)}, u32[]{:S(2)}) collective-permute-start(f32[2,128]{1,0:T(2,128)S(1)} %broadcast_select_fusion.26), channel_id=1, source_target_pairs={{0,2},{1,3},{2,0},{3,1},{4,6},{5,7},{6,4},{7,5},{8,10},{9,11},{10,... | collective-permute-start | bytes 3080 | tf_op jit(solution)/shard_map/ppermute | solution.py:515
  351.9 11.9 %collective-permute-start.47 = (bf16[640,128]{1,0:T(8,128)(2,1)S(1)}, bf16[640,128]{1,0:T(8,128)(2,1)S(1)}, u32[]{:S(2)}, u32[]{:S(2)}) collective-permute-start(bf16[640,128]{1,0:T(8,128)(2,1)S(1)} %get-tuple-element.237), channel_id=1, source_target_pairs={{0,2},{1,3},{2,0},{3,1},{4,6},{5,7},{6,4},{7,5},{8,10},{9,11},{10,... | collective-permute-start | bytes 491528 | tf_op jit(solution)/shard_map/ppermute | solution.py:515
  361.3 8.7 %collective-permute-start.29 = (bf16[512,256]{1,0:T(8,128)(2,1)S(1)}, bf16[512,256]{1,0:T(8,128)(2,1)S(1)}, u32[]{:S(2)}, u32[]{:S(2)}) collective-permute-start(bf16[512,256]{1,0:T(8,128)(2,1)S(1)} %copy-done.45), channel_id=1, source_target_pairs={{0,1},{1,0},{2,3},{3,2},{4,5},{5,4},{6,7},{7,6},{8,9},{9,8},{10,11... | collective-permute-start | bytes 786440 | tf_op jit(solution)/shard_map/ppermute | solution.py:515
  383.6 23.5 %collective-permute-start.34 = (f32[8,256]{1,0:T(8,128)S(1)}, f32[8,256]{1,0:T(8,128)S(1)}, u32[]{:S(2)}, u32[]{:S(2)}) collective-permute-start(f32[8,256]{1,0:T(8,128)S(1)} %slice.215), channel_id=1, source_target_pairs={{0,1},{1,0},{2,3},{3,2},{4,5},{5,4},{6,7},{7,6},{8,9},{9,8},{10,11... | collective-permute-start | bytes 24584 | tf_op jit(solution)/shard_map/ppermute | solution.py:515
  386.7 64.3 %collective-permute-start.49 = (bf16[3328,128]{1,0:T(8,128)(2,1)}, bf16[3328,128]{1,0:T(8,128)(2,1)}, u32[]{:S(2)}, u32[]{:S(2)}) collective-permute-start(bf16[3328,128]{1,0:T(8,128)(2,1)} %fusion.1), channel_id=1, source_target_pairs={{0,4},{4,0},{8,12},{12,8},{16,20},{20,16},{24,28},{28,24},{1,5},{5... | collective-permute-start | bytes 2555912 | tf_op jit(solution)/shard_map/ppermute | solution.py:518
  407.7 10.9 %all-to-all-start.7 = ((f32[8,8,256]{2,1,0:T(8,128)}), f32[8,8,256]{2,1,0:T(8,128)S(1)}, u32[]{:S(2)}, u32[]{:S(2)}) async-start(f32[8,8,256]{2,1,0:T(8,128)} %broadcast_in_dim.29), calls=%async_computation.7 | async-start | bytes 131072 | tf_op jit(solution)/shard_map/all_to_all | solution.py:530
  415.4 11.4 %collective-permute-start.37 = (bf16[640,128]{1,0:T(8,128)(2,1)}, bf16[640,128]{1,0:T(8,128)(2,1)}, u32[]{:S(2)}, u32[]{:S(2)}) collective-permute-start(bf16[640,128]{1,0:T(8,128)(2,1)} %get-tuple-element.239), channel_id=1, source_target_pairs={{0,2},{1,3},{2,0},{3,1},{4,6},{5,7},{6,4},{7,5},{8,10},{9,11},{10,... | collective-permute-start | bytes 491528 | tf_op jit(solution)/shard_map/ppermute | solution.py:515
  416.8 17.0 %collective-permute-start.33 = (bf16[512,256]{1,0:T(8,128)(2,1)}, bf16[512,256]{1,0:T(8,128)(2,1)}, u32[]{:S(2)}, u32[]{:S(2)}) collective-permute-start(bf16[512,256]{1,0:T(8,128)(2,1)} %get-tuple-element.67), channel_id=1, source_target_pairs={{0,1},{1,0},{2,3},{3,2},{4,5},{5,4},{6,7},{7,6},{8,9},{9,8},{10,11... | collective-permute-start | bytes 786440 | tf_op jit(solution)/shard_map/ppermute | solution.py:515
  418.7 18.2 %collective-permute-start.58 = (f32[2,128]{1,0:T(2,128)S(1)}, f32[2,128]{1,0:T(2,128)S(1)}, u32[]{:S(2)}, u32[]{:S(2)}) collective-permute-start(f32[2,128]{1,0:T(2,128)S(1)} %broadcast_select_fusion.22), channel_id=1, source_target_pairs={{0,2},{1,3},{2,0},{3,1},{4,6},{5,7},{6,4},{7,5},{8,10},{9,11},{10,... | collective-permute-start | bytes 3080 | tf_op jit(solution)/shard_map/ppermute | solution.py:515
  433.7 13.6 %collective-permute-start.38 = (bf16[2304,128]{1,0:T(8,128)(2,1)S(1)}, bf16[2304,128]{1,0:T(8,128)(2,1)S(1)}, u32[]{:S(2)}, u32[]{:S(2)}) collective-permute-start(bf16[2304,128]{1,0:T(8,128)(2,1)S(1)} %dynamic-slice_convert_fusion), channel_id=1, source_target_pairs={{0,4},{4,0},{8,12},{12,8},{16,20},{20,16},{24,28},{28,24},{1,5},{5... | collective-permute-start | bytes 1769480 | tf_op jit(solution)/shard_map/ppermute | solution.py:518
  436.9 8.6 %collective-permute-start.35 = (bf16[512,128]{1,0:T(8,128)(2,1)}, bf16[512,128]{1,0:T(8,128)(2,1)S(1)}, u32[]{:S(2)}, u32[]{:S(2)}) collective-permute-start(bf16[512,128]{1,0:T(8,128)(2,1)} %get-tuple-element.71), channel_id=1, source_target_pairs={{0,2},{1,3},{2,0},{3,1},{4,6},{5,7},{6,4},{7,5},{8,10},{9,11},{10,... | collective-permute-start | bytes 393224 | tf_op jit(solution)/shard_map/ppermute | solution.py:515
  447.5 8.8 %collective-permute-start.39 = (bf16[576,128]{1,0:T(8,128)(2,1)S(1)}, bf16[576,128]{1,0:T(8,128)(2,1)S(1)}, u32[]{:S(2)}, u32[]{:S(2)}) collective-permute-start(bf16[576,128]{1,0:T(8,128)(2,1)S(1)} %get-tuple-element.209), channel_id=1, source_target_pairs={{0,24},{4,28},{8,16},{12,20},{16,8},{20,12},{24,0},{28,4},{1,25},{... | collective-permute-start | bytes 442376 | tf_op jit(solution)/shard_map/ppermute | solution.py:518
  450.1 8.3 %collective-permute-start.41 = (bf16[576,128]{1,0:T(8,128)(2,1)S(1)}, bf16[576,128]{1,0:T(8,128)(2,1)S(1)}, u32[]{:S(2)}, u32[]{:S(2)}) collective-permute-start(bf16[576,128]{1,0:T(8,128)(2,1)S(1)} %get-tuple-element.210), channel_id=1, source_target_pairs={{0,16},{4,20},{8,24},{12,28},{16,0},{20,4},{24,8},{28,12},{1,17},{... | collective-permute-start | bytes 442376 | tf_op jit(solution)/shard_map/ppermute | solution.py:518
  450.7 8.1 %collective-permute-start.40 = (bf16[576,128]{1,0:T(8,128)(2,1)S(1)}, bf16[576,128]{1,0:T(8,128)(2,1)S(1)}, u32[]{:S(2)}, u32[]{:S(2)}) collective-permute-start(bf16[576,128]{1,0:T(8,128)(2,1)S(1)} %get-tuple-element.211), channel_id=1, source_target_pairs={{0,8},{4,12},{8,0},{12,4},{16,24},{20,28},{24,16},{28,20},{1,9},{5... | collective-permute-start | bytes 442376 | tf_op jit(solution)/shard_map/ppermute | solution.py:518
  453.1 9.8 %collective-permute-start.50 = (bf16[832,128]{1,0:T(8,128)(2,1)S(1)}, bf16[832,128]{1,0:T(8,128)(2,1)S(1)}, u32[]{:S(2)}, u32[]{:S(2)}) collective-permute-start(bf16[832,128]{1,0:T(8,128)(2,1)S(1)} %get-tuple-element.204), channel_id=1, source_target_pairs={{0,24},{4,28},{8,16},{12,20},{16,8},{20,12},{24,0},{28,4},{1,25},{... | collective-permute-start | bytes 638984 | tf_op jit(solution)/shard_map/ppermute | solution.py:518
  455.7 13.3 %collective-permute-start.52 = (bf16[832,128]{1,0:T(8,128)(2,1)S(1)}, bf16[832,128]{1,0:T(8,128)(2,1)S(1)}, u32[]{:S(2)}, u32[]{:S(2)}) collective-permute-start(bf16[832,128]{1,0:T(8,128)(2,1)S(1)} %get-tuple-element.205), channel_id=1, source_target_pairs={{0,16},{4,20},{8,24},{12,28},{16,0},{20,4},{24,8},{28,12},{1,17},{... | collective-permute-start | bytes 638984 | tf_op jit(solution)/shard_map/ppermute | solution.py:518
  456.3 12.7 %collective-permute-start.51 = (bf16[832,128]{1,0:T(8,128)(2,1)S(1)}, bf16[832,128]{1,0:T(8,128)(2,1)S(1)}, u32[]{:S(2)}, u32[]{:S(2)}) collective-permute-start(bf16[832,128]{1,0:T(8,128)(2,1)S(1)} %get-tuple-element.206), channel_id=1, source_target_pairs={{0,8},{4,12},{8,0},{12,4},{16,24},{20,28},{24,16},{28,20},{1,9},{5... | collective-permute-start | bytes 638984 | tf_op jit(solution)/shard_map/ppermute | solution.py:518
  458.8 13.5 %collective-permute-start.44 = (bf16[576,128]{1,0:T(8,128)(2,1)S(1)}, bf16[576,128]{1,0:T(8,128)(2,1)S(1)}, u32[]{:S(2)}, u32[]{:S(2)}) collective-permute-start(bf16[576,128]{1,0:T(8,128)(2,1)S(1)} %fusion.14), channel_id=1, source_target_pairs={{0,24},{4,28},{8,16},{12,20},{16,8},{20,12},{24,0},{28,4},{1,25},{... | collective-permute-start | bytes 442376 | tf_op jit(solution)/shard_map/ppermute | solution.py:518
  461.1 12.8 %collective-permute-start.43 = (bf16[576,128]{1,0:T(8,128)(2,1)S(1)}, bf16[576,128]{1,0:T(8,128)(2,1)S(1)}, u32[]{:S(2)}, u32[]{:S(2)}) collective-permute-start(bf16[576,128]{1,0:T(8,128)(2,1)S(1)} %fusion.14), channel_id=1, source_target_pairs={{0,16},{4,20},{8,24},{12,28},{16,0},{20,4},{24,8},{28,12},{1,17},{... | collective-permute-start | bytes 442376 | tf_op jit(solution)/shard_map/ppermute | solution.py:518
  462.9 11.3 %collective-permute-start.42 = (bf16[576,128]{1,0:T(8,128)(2,1)S(1)}, bf16[576,128]{1,0:T(8,128)(2,1)S(1)}, u32[]{:S(2)}, u32[]{:S(2)}) collective-permute-start(bf16[576,128]{1,0:T(8,128)(2,1)S(1)} %fusion.14), channel_id=1, source_target_pairs={{0,8},{4,12},{8,0},{12,4},{16,24},{20,28},{24,16},{28,20},{1,9},{5... | collective-permute-start | bytes 442376 | tf_op jit(solution)/shard_map/ppermute | solution.py:518
  469.1 9.4 %collective-permute-start.55 = (bf16[832,128]{1,0:T(8,128)(2,1)S(1)}, bf16[832,128]{1,0:T(8,128)(2,1)S(1)}, u32[]{:S(2)}, u32[]{:S(2)}) collective-permute-start(bf16[832,128]{1,0:T(8,128)(2,1)S(1)} %fusion.11), channel_id=1, source_target_pairs={{0,24},{4,28},{8,16},{12,20},{16,8},{20,12},{24,0},{28,4},{1,25},{... | collective-permute-start | bytes 638984 | tf_op jit(solution)/shard_map/ppermute | solution.py:518
  470.3 11.7 %collective-permute-start.54 = (bf16[832,128]{1,0:T(8,128)(2,1)S(1)}, bf16[832,128]{1,0:T(8,128)(2,1)S(1)}, u32[]{:S(2)}, u32[]{:S(2)}) collective-permute-start(bf16[832,128]{1,0:T(8,128)(2,1)S(1)} %fusion.11), channel_id=1, source_target_pairs={{0,16},{4,20},{8,24},{12,28},{16,0},{20,4},{24,8},{28,12},{1,17},{... | collective-permute-start | bytes 638984 | tf_op jit(solution)/shard_map/ppermute | solution.py:518
  472.3 10.3 %collective-permute-start.53 = (bf16[832,128]{1,0:T(8,128)(2,1)S(1)}, bf16[832,128]{1,0:T(8,128)(2,1)S(1)}, u32[]{:S(2)}, u32[]{:S(2)}) collective-permute-start(bf16[832,128]{1,0:T(8,128)(2,1)S(1)} %fusion.11), channel_id=1, source_target_pairs={{0,8},{4,12},{8,0},{12,4},{16,24},{20,28},{24,16},{28,20},{1,9},{5... | collective-permute-start | bytes 638984 | tf_op jit(solution)/shard_map/ppermute | solution.py:518
  474.5 8.4 %collective-permute-start.45 = (bf16[2304,128]{1,0:T(8,128)(2,1)S(1)}, bf16[2304,128]{1,0:T(8,128)(2,1)S(1)}, u32[]{:S(2)}, u32[]{:S(2)}) collective-permute-start(bf16[2304,128]{1,0:T(8,128)(2,1)S(1)} %pad_maximum_fusion.6), channel_id=1, source_target_pairs={{0,4},{4,0},{8,12},{12,8},{16,20},{20,16},{24,28},{28,24},{1,5},{5... | collective-permute-start | bytes 1769480 | tf_op jit(solution)/shard_map/ppermute | solution.py:518
  (66 other events, 713.2 us)
Sparse Core Ops, SparseCore 0:
  44.5 24.1 all-gather.7
  71.1 25.5 all-gather.9
  252.0 24.7 all-gather.11
Sparse Core Ops, SparseCore 1:
  150.6 20.1 reduce-scatter.3
